TPU v7x, 512 devices: a whole 4x8x8 slice. The times are simulated.
512 devices in a mesh: mirror: 32 (over y, z_hi, core), blk: 16 (over x, z_lo).
Axes of the slice: x: 4, y: 8, z: 8 (z_hi: 2, z_lo: 4; z = z_hi * 4 + z_lo), core: 2. Of those that a mesh axis runs over, the one named last changes fastest.
Arguments:
- colloc: float32 [4096, 2048], P('blk'), may hold values from -2 to 2
- coeffs: float32 [128, 4096], P('blk'), may hold values from -6 to 6
- targets: float32 [32, 128, 128, 128], P('mirror', 'blk'), may hold values from -6 to 6
- pair_list: int32 [32, 2], P('mirror'), may hold values from 0 to 15, as said below
Outputs:
- residual: float32 [32, 128, 128, 128], P('mirror', 'blk')
- gradient: float32 [128, 4096], P('blk', 'mirror')
Inputs may be any that keep to these rules, and one draw needn't show every extreme that they name: `pair_list`: p != q in every row, and for m < 16 row m + 16 holds the row m reversed, (q, p).
All inputs are finite; a program needn't handle non-finite values.
Results may differ from a plain program's by a relative error of at most 0.0003.
Values sent between devices are 32-bit elements; how exact they have to be, the bound alone decides.
No kernel may reach another device: no remote copies, remote signals or barrier semaphores. Data moves between devices by JAX's collectives and lax.ppermute only.
A program may use at most 64 MiB of HBM per device.

v0:
```python
import jax
import jax.numpy as jnp
from jax import lax
from jax.sharding import PartitionSpec as P

highest = lax.Precision.HIGHEST


def from_behind(x, axis, by):
    devices = lax.axis_size(axis)
    return lax.ppermute(x, axis, [(i, (i + by) % devices) for i in range(devices)])


def project_rows(coef_rows, row_block, block_width):
    weighted = coef_rows[:, :, None] * row_block[None, :, :block_width]
    return jnp.einsum("agp,gq->apq", weighted, row_block[:, block_width:], precision=highest)


def spread_rows(misfit, row_block, block_width):
    spread = jnp.einsum("gp,apq->agq", row_block[:, :block_width], misfit, precision=highest)
    return jnp.sum(spread * row_block[None, :, block_width:], axis=2)


def step_length():
    return 512


def fold_project(running_sum, row_block, coef_rows, block_width):
    row_count = row_block.shape[0]
    size_step = step_length()
    block_count = row_count // size_step
    stacked_rows = row_block.reshape(block_count, size_step, row_block.shape[1])
    stacked_coef = jnp.moveaxis(coef_rows.reshape(coef_rows.shape[0], block_count, size_step), 1, 0)

    def step_fn(partial_sum, block_item):
        return (partial_sum + project_rows(block_item[0], block_item[1], block_width), None)

    result, unused = lax.scan(step_fn, running_sum, (stacked_coef, stacked_rows))
    return result


def map_spread(misfit, row_block, block_width):
    row_count = row_block.shape[0]
    size_step = step_length()
    block_count = row_count // size_step
    stacked_rows = row_block.reshape(block_count, size_step, row_block.shape[1])
    pieces = lax.map(lambda one_rows: spread_rows(misfit, one_rows, block_width), stacked_rows)
    return jnp.moveaxis(pieces, 0, 1).reshape(misfit.shape[0], row_count)


def per_device(colloc, coeffs, targets, pair_list):
    block_width = targets.shape[-1]
    left_cols = lax.dynamic_slice_in_dim(colloc, pair_list[0, 0] * block_width, block_width, 1)
    right_cols = lax.dynamic_slice_in_dim(colloc, pair_list[0, 1] * block_width, block_width, 1)
    paired = jnp.concatenate([left_cols, right_cols], axis=1)
    shift_by = lax.axis_size("mirror") // 2
    mirrored = from_behind(targets, "mirror", shift_by)
    symmetric = 0.5 * (targets[0] + jnp.swapaxes(mirrored[0], 1, 2))
    zero_fit = jnp.zeros((targets.shape[1], block_width, block_width), jnp.float32)
    gathered = lax.all_gather(paired, "blk", axis=0, tiled=True)
    fitted = fold_project(zero_fit, gathered, coeffs, block_width)
    residual = symmetric - fitted
    misfit = targets[0] - fitted
    grid_terms = map_spread(misfit, gathered, block_width)
    gradient = lax.psum_scatter(grid_terms, "mirror", scatter_dimension=1, tiled=True)
    return (residual[None], gradient)


def solution(mesh):
    return jax.shard_map(
        per_device,
        mesh=mesh,
        in_specs=(
            P("blk", None),
            P("blk", None),
            P("mirror", "blk", None, None),
            P("mirror", None),
        ),
        out_specs=(P("mirror", "blk", None, None), P("blk", "mirror")),
        check_vma=False,
    )
```

profile of v0, /device:TPU:1, one launch (start us, length us, event | category | flops | bytes accessed | tf_op | source)
XLA Modules:
  0.0 303.7 jit_solution(5931016419976223859)
XLA Ops:
  7.2 1.3 fusion.12
  11.5 1.2 copy.8
  12.8 8.3 %collective-permute-start = (f32[1,8,128,128]{2,3,1,0:T(8,128)S(1)}, f32[1,8,128,128]{2,3,1,0:T(8,128)S(1)}, u32[]{:S(2)}, u32[]{:S(2)}) collective-permute-start(f32[1,8,128,128]{2,3,1,0:T(8,128)S(1)} %copy.8), channel_id=1, source_target_pairs={{0,256},{16,272},{32,288},{48,304},{64,320},{80,336},{96,352},{112... | collective-permute-start | bytes 1572872 | tf_op jit(solution)/shard_map/ppermute | solution.py:11
  21.1 100.8 %all-gather.2.cloned.1.call-done = f32[4096,256]{1,0:T(8,128)} async-done(((f32[256,256]{1,0:T(8,128)}), f32[4096,256]{1,0:T(8,128)}) %all-gather.2.cloned.1.call-update) | async-done | bytes 4194320 | tf_op jit(solution)/shard_map/all_gather | solution.py:60
  121.9 31.8 %while.22 = (s32[]{:T(128)}, f32[8,128,128]{2,1,0:T(8,128)S(1)}, f32[8,8,512]{2,1,0:T(8,128)}, f32[8,512,256]{2,1,0:T(8,128)}, s32[]{:T(128)}, /*index=5*/s32[]{:T(128)}) while((s32[]{:T(128)}, f32[8,128,128]{2,1,0:T(8,128)S(1)}, f32[8,8,512]{2,1,0:T(8,128)}, f32[8,512,256]{2,1,0:T(8,128)}, s32[]{:T(128)}, ...), condition=%wide.region_1.2_spmd.clone, body=%wide.region_0.1_spmd.clone.sunk | while | flops 806092800 | bytes 3719255 | solution.py:38
  121.9 1.1 dynamic-slice_bitcast_fusion.7
  124.0 2.0 fusion.19
  127.9 2.0 fusion.19
  131.9 2.0 fusion.19
  135.9 2.0 fusion.19
  139.8 2.0 fusion.19
  143.8 2.0 fusion.19
  147.8 2.0 fusion.19
  151.8 2.0 fusion.19
  154.9 29.8 %while.21 = (s32[]{:T(128)}, f32[8,8,512]{2,1,0:T(8,128)}, f32[8,512,256]{2,1,0:T(8,128)}, f32[8,128,128]{1,2,0:T(8,128)S(1)}, s32[]{:T(128)}) while((s32[]{:T(128)}, f32[8,8,512]{2,1,0:T(8,128)}, f32[8,512,256]{2,1,0:T(8,128)}, f32[8,128,128]{1,2,0:T(8,128)S(1)}, s32[]{:T(128)}) %tuple.54), condition=%wide.region_4.5_spmd, body=%wide.region_2.4_spmd.sunk | while | flops 806350848 | bytes 3195457 | solution.py:47
  156.1 1.9 multiply_reduce_fusion.2
  159.9 1.9 multiply_reduce_fusion.2
  163.6 1.9 multiply_reduce_fusion.2
  167.3 1.9 multiply_reduce_fusion.2
  171.0 1.9 multiply_reduce_fusion.2
  174.7 1.9 multiply_reduce_fusion.2
  178.5 1.9 multiply_reduce_fusion.2
  182.2 1.9 multiply_reduce_fusion.2
  184.7 112.2 %reduce-scatter.2.cloned.1.call-done = f32[8,128]{1,0:T(8,128)} async-done(((f32[8,4096]{1,0:T(8,128)}), f32[8,128]{1,0:T(8,128)}) %reduce-scatter.2.cloned.1.call-update) | async-done | bytes 4112 | tf_op jit(solution)/shard_map/reduce_scatter | solution.py:65
  (76 shorter events, 32.1 us)
Async XLA Ops:
  7.2 114.8 %all-gather.2.cloned.1.call-start = ((), (), s32[]{:S(2)}) async-start(), calls=%async_computation.1 | async-start | bytes 4456448 | tf_op jit(solution)/shard_map/all_gather | solution.py:60
  11.5 285.4 %reduce-scatter.2.cloned.1.call-start = ((), (), s32[]{:S(2)}) async-start(), calls=%async_computation.2 | async-start | bytes 135168 | tf_op jit(solution)/shard_map/reduce_scatter | solution.py:65
  12.8 141.0 %collective-permute-start = (f32[1,8,128,128]{2,3,1,0:T(8,128)S(1)}, f32[1,8,128,128]{2,3,1,0:T(8,128)S(1)}, u32[]{:S(2)}, u32[]{:S(2)}) collective-permute-start(f32[1,8,128,128]{2,3,1,0:T(8,128)S(1)} %copy.8), channel_id=1, source_target_pairs={{0,256},{16,272},{32,288},{48,304},{64,320},{80,336},{96,352},{112... | collective-permute-start | bytes 1572872 | tf_op jit(solution)/shard_map/ppermute | solution.py:11
  121.9 31.9 %copy-start = (f32[1,8,128,128]{3,2,1,0:T(8,128)S(1)}, f32[1,8,128,128]{3,2,1,0:T(8,128)}, u32[]{:S(2)}) copy-start(f32[1,8,128,128]{3,2,1,0:T(8,128)} %param.10) | copy-start | bytes 1572868
Sparse Core Ops, SparseCore 0:
  11.6 110.2 all-gather.1
  184.8 112.0 reduce-scatter.1
where the time goes:
time: 310 us; the launch traced here: 304 us
  waiting for transfers between devices  213 us (69%)
  local copies, waits for them, and re-layouts  34 us (11%)
  matrix products  30.8 us (10%)
  between operations  15.3 us (5%)
  starting transfers between devices  8.36 us (3%)
    reduce_scatter x1, waiting for transfers between devices, per_device(): lax.psum_scatter(grid_terms, 'mirror', scatter_dimension=1, tiled=True)  112 us
    all_gather x1, waiting for transfers between devices, per_device(): gathered = lax.all_gather(paired, 'blk', axis=0, tiled=True)  101 us
    squeeze x16, local copies, waits for them, and re-layouts, fold_project(): lax.scan(step_fn, running_sum, (stacked_coef, stacked_rows))  17.3 us
    dot_general x8, matrix products, project_rows(): jnp.einsum('agp,gq->apq', weighted, row_block[:, block_width:], precision...  15.8 us
    while x8, matrix products  14.9 us
    ppermute x1, starting transfers between devices, from_behind(): lax.ppermute(x, axis, [(i, (i + by) % devices) for i in range(devices)])  8.28 us
  transfers between devices with their start and end apart: 3, of which 2 were waited for; matrix products, arithmetic and copies ran while one was open for 11% of the time, Pallas kernels for 0%

commit v1 on v0

v1 whole, which is shorter than its diff:
```python
import jax
import jax.numpy as jnp
from jax import lax
from jax.experimental import pallas as pl
from jax.experimental.pallas import tpu as pltpu
from jax.sharding import PartitionSpec as P

NX, NZ = 4, 4
NY, NZH, NC = 8, 2, 2
MIRROR = NY * NZH * NC
HALF = MIRROR // 2
bf16, f32 = jnp.bfloat16, jnp.float32
VMEM = pl.BlockSpec(memory_space=pltpu.VMEM)
SMEM = pl.BlockSpec(memory_space=pltpu.SMEM)
ANY = pl.BlockSpec(memory_space=pl.ANY)


def params(mib=32):
    return pltpu.CompilerParams(vmem_limit_bytes=mib * 1024 * 1024)


def swap_pairs():
    out = []
    for m in range(MIRROR):
        low = m < HALF
        if low and m % 2 == 1:
            out.append((m, m + HALF - 1))
        elif not low and m % 2 == 0:
            out.append((m, m - HALF + 1))
        else:
            out.append((m, m))
    return out


def x_shift(by):
    return [(x * NZ + z, ((x + by) % NX) * NZ + z) for x in range(NX) for z in range(NZ)]


def split(v):
    hi = v.astype(bf16)
    return hi, (v - hi.astype(f32)).astype(bf16)


def pick_kernel(mine_ref, mate_ref, colloc_ref, out_ref, sems):
    m = lax.axis_index("mirror")
    core = lax.rem(m, 2)
    low = (m < HALF).astype(jnp.int32)
    keeps = core != low
    p = jnp.where(keeps, mine_ref[0, 0], mate_ref[0, 1])
    q = jnp.where(keeps, mine_ref[0, 1], mate_ref[0, 0])
    n = out_ref.shape[0]
    row = pl.multiple_of(core * n, n)
    copies = []
    for k, block in enumerate((p, q)):
        copies.append(
            pltpu.make_async_copy(
                colloc_ref.at[pl.ds(row, n), pl.ds(pl.multiple_of(block * 128, 128), 128)],
                out_ref.at[:, pl.ds(k * 128, 128)],
                sems.at[k],
            )
        )
    for c in copies:
        c.start()
    for c in copies:
        c.wait()


def fit_kernel(own_ref, below_ref, above_ref, opp0_ref, opp1_ref, coef_ref, t_ref, u_ref, lt_ref, rt_ref, whi, wlo, acc):
    core = lax.rem(lax.axis_index("mirror"), 2)
    x = lax.axis_index("blk") // NZ
    naux = coef_ref.shape[0]
    sources = (
        (0, (own_ref,)),
        (NX - 1, (below_ref,)),
        (1, (above_ref,)),
        (2, (opp0_ref, opp1_ref)),
    )
    for n, (dx, refs) in enumerate(sources):
        xs = lax.rem(x + dx, NX)
        rows = jnp.concatenate([r[...] for r in refs], axis=0) if len(refs) > 1 else refs[0][...]
        left, right = rows[:, :128], rows[:, 128:]
        lt, rt = left.T, right.T
        lt_ref[:, pl.ds(n * 512, 512)] = lt
        rhi, rlo = split(right)
        rthi, rtlo = split(rt)
        rt_ref[0:128, pl.ds(n * 512, 512)] = rthi
        rt_ref[128:256, pl.ds(n * 512, 512)] = rtlo
        both = jnp.concatenate([rhi, rlo], axis=1)
        cs = []
        for z in range(NZ):
            at = pl.multiple_of((xs * NZ + z) * 256 + core * 128, 128)
            cs.append(coef_ref[:, pl.ds(at, 128)])
        cf = jnp.concatenate(cs, axis=1)
        for a in range(naux):
            hi, lo = split(cf[a : a + 1, :] * lt)
            whi[pl.ds(a * 128, 128), :] = hi
            wlo[pl.ds(a * 128, 128), :] = lo
        part = jnp.dot(whi[...], both, preferred_element_type=f32)
        part += jnp.dot(wlo[...], both, preferred_element_type=f32)
        if n == 0:
            acc[...] = part
        elif n < len(sources) - 1:
            acc[...] += part
        else:
            tot = acc[...] + part
            fit = tot[:, :128] + tot[:, 128:]
            u_ref[...] = 0.5 * t_ref[...] - fit.reshape(naux, 128, 128)


def residual_kernel(u_ref, o_ref, r_ref):
    for a in range(u_ref.shape[0]):
        r_ref[a] = u_ref[a] + o_ref[a].T


def gradient_kernel(r_ref, lt_ref, rt_ref, keep_ref, send_ref, hh, ll, parts):
    m = lax.axis_index("mirror")
    zh = lax.rem(m // NC, NZH)
    x = lax.axis_index("blk") // NZ
    naux = r_ref.shape[0]
    for a in range(naux):
        hi, lo = split(2.0 * r_ref[a])
        hh[pl.ds(a * 128, 128), 0:128] = hi
        hh[pl.ds(a * 128, 128), 128:256] = hi
        ll[pl.ds(a * 128, 128), 0:128] = lo
        ll[pl.ds(a * 128, 128), 128:256] = lo
    for n, dx in enumerate((0, NX - 1, 1, 2)):
        xs = lax.rem(x + dx, NX)
        for h in range(2):
            cols = pl.ds(n * 512 + h * 256, 256)
            rt = rt_ref[:, cols]
            spread = jnp.dot(hh[...], rt, preferred_element_type=f32)
            spread += jnp.dot(ll[...], rt, preferred_element_type=f32)
            lt = lt_ref[:, cols]
            terms = []
            for a in range(naux):
                terms.append(jnp.sum(spread[a * 128 : (a + 1) * 128] * lt, axis=0, keepdims=True))
            block = jnp.concatenate(terms, axis=0)
            for z in range(2):
                parts[xs * NZ + h * 2 + z] = block[:, z * 128 : (z + 1) * 128]
    for y in range(NY):
        keep_ref[y] = parts[y * NZH + zh]
        send_ref[y] = parts[y * NZH + 1 - zh]


def per_device(colloc, coeffs, targets, pair_list):
    naux, nb = targets.shape[1], targets.shape[2]
    mate = lax.ppermute(pair_list, "mirror", [(m, m ^ 1) for m in range(MIRROR)])
    work = lax.ppermute(targets, "mirror", swap_pairs())[0]

    rows = pl.pallas_call(
        pick_kernel,
        out_shape=jax.ShapeDtypeStruct((colloc.shape[0] // 2, 2 * nb), f32),
        in_specs=[SMEM, SMEM, ANY],
        out_specs=VMEM,
        scratch_shapes=[pltpu.SemaphoreType.DMA((2,))],
        compiler_params=params(8),
        name="pick",
    )(pair_list, mate, colloc)

    z_groups = [[x * NZ + z for z in range(NZ)] for x in range(NX)]
    own = lax.all_gather(rows, "blk", axis=0, tiled=True, axis_index_groups=z_groups)
    below = lax.ppermute(own, "blk", x_shift(1))
    above = lax.ppermute(own, "blk", x_shift(-1))
    h = own.shape[0] // 2
    opp0 = lax.ppermute(below[:h], "blk", x_shift(1))
    opp1 = lax.ppermute(above[h:], "blk", x_shift(-1))

    u, lt, rt = pl.pallas_call(
        fit_kernel,
        out_shape=(
            jax.ShapeDtypeStruct((naux, nb, nb), f32),
            jax.ShapeDtypeStruct((nb, 2048), f32),
            jax.ShapeDtypeStruct((2 * nb, 2048), bf16),
        ),
        in_specs=[VMEM] * 7,
        out_specs=[VMEM] * 3,
        scratch_shapes=[
            pltpu.VMEM((naux * nb, 512), bf16),
            pltpu.VMEM((naux * nb, 512), bf16),
            pltpu.VMEM((naux * nb, 2 * nb), f32),
        ],
        compiler_params=params(),
        cost_estimate=pl.CostEstimate(flops=4 * 2 * 1024 * 2048 * 128, bytes_accessed=6 << 20, transcendentals=0),
        name="fit",
    )(own, below, above, opp0, opp1, coeffs, work)

    other = lax.ppermute(u, "mirror", [(m, m ^ 1) for m in range(MIRROR)])
    res = pl.pallas_call(
        residual_kernel,
        out_shape=jax.ShapeDtypeStruct((naux, nb, nb), f32),
        in_specs=[VMEM] * 2,
        out_specs=VMEM,
        compiler_params=params(16),
        cost_estimate=pl.CostEstimate(flops=1 << 17, bytes_accessed=3 << 19, transcendentals=0),
        name="residual",
    )(u, other)
    residual = lax.ppermute(res[None], "mirror", swap_pairs())

    keep, send = pl.pallas_call(
        gradient_kernel,
        out_shape=(jax.ShapeDtypeStruct((NY, naux, nb), f32),) * 2,
        in_specs=[VMEM] * 3,
        out_specs=[VMEM] * 2,
        scratch_shapes=[
            pltpu.VMEM((naux * nb, 2 * nb), bf16),
            pltpu.VMEM((naux * nb, 2 * nb), bf16),
            pltpu.VMEM((NX * NZ, naux, nb), f32),
        ],
        compiler_params=params(),
        cost_estimate=pl.CostEstimate(flops=4 * 2 * 1024 * 2048 * 128, bytes_accessed=4 << 20, transcendentals=0),
        name="gradient",
    )(res, lt, rt)
    flip = [(m, m ^ NC) for m in range(MIRROR)]
    half_sum = keep + lax.ppermute(send, "mirror", flip)
    y_groups = [[(y * NZH + h) * NC + c for y in range(NY)] for h in range(NZH) for c in range(NC)]
    spread = lax.all_to_all(half_sum, "mirror", 0, 0, tiled=True, axis_index_groups=y_groups)
    return residual, jnp.sum(spread, axis=0)


def solution(mesh):
    return jax.shard_map(
        per_device,
        mesh=mesh,
        in_specs=(
            P("blk", None),
            P("blk", None),
            P("mirror", "blk", None, None),
            P("mirror", None),
        ),
        out_specs=(P("mirror", "blk", None, None), P("blk", "mirror")),
        check_vma=False,
    )
```

time: 310 us -> 93.3 us (0.30); the launches traced: 304 us -> 92.9 us
  waiting for transfers between devices: 213 us -> 11.1 us
  starting transfers between devices: 8.36 us -> 49.3 us
  local copies, waits for them, and re-layouts: 34 us -> 3.08 us
  matrix products: 30.8 us -> 0 us
  blocking collectives: 0 us -> 22.3 us
  between operations: 15.3 us -> 0.78 us
  Pallas kernels: 0 us -> 5.67 us
    reduce_scatter x1 -> x0, waiting for transfers between devices: 112 us -> none  [per_device(): lax.psum_scatter(grid_terms, 'mirror', scatter_dimension=1, tiled=True)]
    all_gather x1 -> x0, waiting for transfers between devices: 101 us -> none  [per_device(): gathered = lax.all_gather(paired, 'blk', axis=0, tiled=True)]
    ppermute x1 -> x9, starting transfers between devices: 8.28 us -> 49.3 us  [the longest x1 9.16 us: per_device(): work = lax.ppermute(targets, 'mirror', swap_pairs())[0]]
    squeeze x16 -> x0, local copies, waits for them, and re-layouts: 17.3 us -> none  [fold_project(): lax.scan(step_fn, running_sum, (stacked_coef, stacked_rows))]
    dot_general x8 -> x0, matrix products: 15.8 us -> none  [project_rows(): jnp.einsum('agp,gq->apq', weighted, row_block[:, block_width:], precision...]
    while x8 -> x0, matrix products: 14.9 us -> none
    all_gather x0 -> x1, blocking collectives: none -> 13.1 us  [per_device(): lax.all_gather(rows, 'blk', axis=0, tiled=True, axis_index_groups=z_groups)]
    ppermute x1 -> x9, waiting for transfers between devices: 0.01 us -> 11.1 us  [the longest x1 5.08 us: per_device(): opp0 = lax.ppermute(below[:h], 'blk', x_shift(1))]
  transfers between devices with their start and end apart: 3 -> 9, of which waited for: 2 -> 6; matrix products, arithmetic and copies ran while one was open for 11% -> 1% of each run, Pallas kernels for 0% -> 3%
where the time goes in v1:
time: 93.3 us; the launch traced here: 92.9 us
  starting transfers between devices  49.3 us (53%)
  blocking collectives  22.3 us (24%)
  waiting for transfers between devices  11.1 us (12%)
  Pallas kernels  5.67 us (6%)
  local copies, waits for them, and re-layouts  3.08 us (3%)
    all_gather x1, blocking collectives, per_device(): lax.all_gather(rows, 'blk', axis=0, tiled=True, axis_index_groups=z_groups)  13.1 us
    all_to_all x1, blocking collectives, per_device(): lax.all_to_all(half_sum, 'mirror', 0, 0, tiled=True, axis_index_groups=y_...  9.26 us
    ppermute x1, starting transfers between devices, per_device(): work = lax.ppermute(targets, 'mirror', swap_pairs())[0]  9.16 us
    ppermute x1, starting transfers between devices, per_device(): lax.ppermute(pair_list, 'mirror', [(m, m ^ 1) for m in range(MIRROR)])  8.79 us
    ppermute x1, starting transfers between devices, per_device(): half_sum = keep + lax.ppermute(send, 'mirror', flip)  7.94 us
    ppermute x1, starting transfers between devices, per_device(): residual = lax.ppermute(res[None], 'mirror', swap_pairs())  6.95 us
    ppermute x1, waiting for transfers between devices, per_device(): opp0 = lax.ppermute(below[:h], 'blk', x_shift(1))  5.08 us
    ppermute x1, starting transfers between devices, per_device(): opp1 = lax.ppermute(above[h:], 'blk', x_shift(-1))  4.85 us
  transfers between devices with their start and end apart: 9, of which 6 were waited for; matrix products, arithmetic and copies ran while one was open for 1% of the time, Pallas kernels for 3%

profile of v1, /device:TPU:1, one launch (start us, length us, event | category | flops | bytes accessed | tf_op | source)
XLA Modules:
  0.0 92.9 jit_solution(3810145439976468724)
XLA Ops:
  0.6 8.8 %collective-permute-start = (s32[1,2]{1,0:T(1,128)}, s32[1,2]{1,0:T(1,128)S(1)}, u32[]{:S(2)}, u32[]{:S(2)}) collective-permute-start(s32[1,2]{1,0:T(1,128)} %mine_ref.1), channel_id=1, source_target_pairs={{0,16},{16,0},{32,48},{48,32},{64,80},{80,64},{96,112},{112,96},{1... | collective-permute-start | bytes 32 | tf_op jit(solution)/shard_map/ppermute | solution.py:147
  9.4 0.9 %collective-permute-done.mate_ref = s32[1,2]{1,0:T(1,128)S(1)} collective-permute-done((s32[1,2]{1,0:T(1,128)}, s32[1,2]{1,0:T(1,128)S(1)}, u32[]{:S(2)}, u32[]{:S(2)}) %collective-permute-start) | collective-permute-done | bytes 40 | tf_op jit(solution)/shard_map/ppermute | solution.py:147
  10.4 1.6 %copy-done = f32[256,2048]{1,0:T(8,128)S(1)} copy-done((f32[256,2048]{1,0:T(8,128)S(1)}, f32[256,2048]{1,0:T(8,128)}, u32[]{:S(2)}) %copy-start) | copy-done | bytes 2097176
  11.9 0.7 copy-done.1
  12.6 0.6 pick.1
  13.2 13.1 %all_gather.3.own_ref = f32[512,256]{1,0:T(8,128)S(1)} all-gather(f32[128,256]{1,0:T(8,128)S(1)} %pick.1), channel_id=1, replica_groups={{0,1,2,3},{4,5,6,7},{8,9,10,11},{12,13,14,15},{16,17,18,19},{20,21,22,2..., dimensions={0}, use_global_device_ids=true | all-gather | bytes 655360 | tf_op jit(solution)/shard_map/all_gather | solution.py:161
  26.3 3.2 %collective-permute-start.2 = (f32[512,256]{1,0:T(8,128)S(1)}, f32[512,256]{1,0:T(8,128)S(1)}, u32[]{:S(2)}, u32[]{:S(2)}) collective-permute-start(f32[512,256]{1,0:T(8,128)S(1)} %all_gather.3.own_ref), channel_id=1, source_target_pairs={{0,12},{1,13},{2,14},{3,15},{4,0},{5,1},{6,2},{7,3},{8,4},{9,5},{1... | collective-permute-start | bytes 1572872 | tf_op jit(solution)/shard_map/ppermute | solution.py:163
  29.5 2.1 %collective-permute-start.1 = (f32[512,256]{1,0:T(8,128)S(1)}, f32[512,256]{1,0:T(8,128)S(1)}, u32[]{:S(2)}, u32[]{:S(2)}) collective-permute-start(f32[512,256]{1,0:T(8,128)S(1)} %all_gather.3.own_ref), channel_id=1, source_target_pairs={{0,4},{1,5},{2,6},{3,7},{4,8},{5,9},{6,10},{7,11},{8,12},{9,13},{1... | collective-permute-start | bytes 1572872 | tf_op jit(solution)/shard_map/ppermute | solution.py:162
  31.6 9.2 %collective-permute-start.5 = (f32[1,8,128,128]{3,2,1,0:T(8,128)S(1)}, f32[1,8,128,128]{3,2,1,0:T(8,128)S(1)}, u32[]{:S(2)}, u32[]{:S(2)}) collective-permute-start(f32[1,8,128,128]{3,2,1,0:T(8,128)S(1)} %copy-done.3), channel_id=1, source_target_pairs={{0,0},{16,256},{32,32},{48,288},{64,64},{80,320},{96,96},{112,352}... | collective-permute-start | bytes 1572872 | tf_op jit(solution)/shard_map/ppermute | solution.py:148
  40.8 4.9 %collective-permute-start.4 = (f32[256,256]{1,0:T(8,128)S(1)}, f32[256,256]{1,0:T(8,128)S(1)}, u32[]{:S(2)}, u32[]{:S(2)}) collective-permute-start(f32[256,256]{1,0:T(8,128)S(1)} %slice.9), channel_id=1, source_target_pairs={{0,12},{1,13},{2,14},{3,15},{4,0},{5,1},{6,2},{7,3},{8,4},{9,5},{1... | collective-permute-start | bytes 786440 | tf_op jit(solution)/shard_map/ppermute | solution.py:166
  45.7 1.9 %collective-permute-start.3 = (f32[256,256]{1,0:T(8,128)S(1)}, f32[256,256]{1,0:T(8,128)S(1)}, u32[]{:S(2)}, u32[]{:S(2)}) collective-permute-start(f32[256,256]{1,0:T(8,128)S(1)} %slice.8), channel_id=1, source_target_pairs={{0,4},{1,5},{2,6},{3,7},{4,8},{5,9},{6,10},{7,11},{8,12},{9,13},{1... | collective-permute-start | bytes 786440 | tf_op jit(solution)/shard_map/ppermute | solution.py:165
  47.6 1.8 %collective-permute-done.5 = f32[1,8,128,128]{3,2,1,0:T(8,128)S(1)} collective-permute-done((f32[1,8,128,128]{3,2,1,0:T(8,128)S(1)}, f32[1,8,128,128]{3,2,1,0:T(8,128)S(1)}, u32[]{:S(2)}, u32[]{:S(2)}) %collective-permute-start.5) | collective-permute-done | bytes 524320 | tf_op jit(solution)/shard_map/ppermute | solution.py:148
  49.5 0.5 collective-permute-done.4.opp1_ref
  49.9 5.1 %collective-permute-done.3.opp0_ref = f32[256,256]{1,0:T(8,128)S(1)} collective-permute-done((f32[256,256]{1,0:T(8,128)S(1)}, f32[256,256]{1,0:T(8,128)S(1)}, u32[]{:S(2)}, u32[]{:S(2)}) %collective-permute-start.3) | collective-permute-done | bytes 262176 | tf_op jit(solution)/shard_map/ppermute | solution.py:165
  55.0 2.5 %fit.1 = (f32[8,128,128]{2,1,0:T(8,128)S(1)}, f32[128,2048]{1,0:T(8,128)S(1)}, bf16[256,2048]{1,0:T(8,128)(2,1)S(1)}) custom-call(f32[512,256]{1,0:T(8,128)S(1)} %all_gather.3.own_ref, f32[512,256]{1,0:T(8,128)S(1)} %collective-permute-done.1.below_ref, f32[512,256]{1,0:T(8,128)S(1)} %collective-permute-done.2.above_ref, ...), custom_call_target="tpu_custom_call" | custom-call | flops 2147483648 | bytes 6291456 | tf_op jit(solution)/shard_map/fit/pallas_call | solution.py:168
  57.5 4.4 %collective-permute-start.6 = (f32[8,128,128]{2,1,0:T(8,128)S(1)}, f32[8,128,128]{2,1,0:T(8,128)S(1)}, u32[]{:S(2)}, u32[]{:S(2)}) collective-permute-start(f32[8,128,128]{2,1,0:T(8,128)S(1)} %get-tuple-element.7.u_ref), channel_id=1, source_target_pairs={{0,16},{16,0},{32,48},{48,32},{64,80},{80,64},{96,112},{112,96},{1... | collective-permute-start | bytes 1572872 | tf_op jit(solution)/shard_map/ppermute | solution.py:187
  61.9 1.5 %collective-permute-done.6.o_ref = f32[8,128,128]{2,1,0:T(8,128)S(1)} collective-permute-done((f32[8,128,128]{2,1,0:T(8,128)S(1)}, f32[8,128,128]{2,1,0:T(8,128)S(1)}, u32[]{:S(2)}, u32[]{:S(2)}) %collective-permute-start.6) | collective-permute-done | bytes 524320 | tf_op jit(solution)/shard_map/ppermute | solution.py:187
  63.7 7.0 %collective-permute-start.7 = (f32[1,8,128,128]{3,2,1,0:T(8,128)S(1)}, f32[1,8,128,128]{3,2,1,0:T(8,128)S(1)}, u32[]{:S(2)}, u32[]{:S(2)}) collective-permute-start(f32[1,8,128,128]{3,2,1,0:T(8,128)S(1)} %bitcast.2), channel_id=1, source_target_pairs={{0,0},{16,256},{32,32},{48,288},{64,64},{80,320},{96,96},{112,352}... | collective-permute-start | bytes 1572872 | tf_op jit(solution)/shard_map/ppermute | solution.py:197
  70.6 2.4 %gradient.1 = (f32[8,8,128]{2,1,0:T(8,128)S(1)}, f32[8,8,128]{2,1,0:T(8,128)S(1)}) custom-call(f32[8,128,128]{2,1,0:T(8,128)S(1)} %residual.1.r_ref, f32[128,2048]{1,0:T(8,128)S(1)} %get-tuple-element.8.lt_ref, bf16[256,2048]{1,0:T(8,128)(2,1)S(1)} %get-tuple-element.9.rt_ref), custom_call_target="tpu_custom_call" | custom-call | flops 2147483648 | bytes 4194304 | tf_op jit(solution)/shard_map/gradient/pallas_call | solution.py:199
  73.0 7.9 %collective-permute-start.8 = (f32[8,8,128]{2,1,0:T(8,128)S(1)}, f32[8,8,128]{2,1,0:T(8,128)S(1)}, u32[]{:S(2)}, u32[]{:S(2)}) collective-permute-start(f32[8,8,128]{2,1,0:T(8,128)S(1)} %get-tuple-element.11), channel_id=1, source_target_pairs={{0,32},{16,48},{32,0},{48,16},{64,96},{80,112},{96,64},{112,80},{1... | collective-permute-start | bytes 98312 | tf_op jit(solution)/shard_map/ppermute | solution.py:214
  81.0 1.3 %collective-permute-done.8 = f32[8,8,128]{2,1,0:T(8,128)S(1)} collective-permute-done((f32[8,8,128]{2,1,0:T(8,128)S(1)}, f32[8,8,128]{2,1,0:T(8,128)S(1)}, u32[]{:S(2)}, u32[]{:S(2)}) %collective-permute-start.8) | collective-permute-done | bytes 32800 | tf_op jit(solution)/shard_map/ppermute | solution.py:214
  82.3 9.3 %all_to_all.5 = f32[8,8,128]{2,1,0:T(8,128)S(1)} all-to-all(f32[8,8,128]{2,1,0:T(8,128)S(1)} %add.3), channel_id=1, replica_groups={{0,64,128,192,256,320,384,448},{16,80,144,208,272,336,400,464},{32,96,1..., dimensions={0} | all-to-all | bytes 65536 | tf_op jit(solution)/shard_map/all_to_all | solution.py:216
  91.5 0.6 reduce_sum.9
  92.1 0.8 copy.7
  (13 shorter events, 0.3 us)
Async XLA Ops:
  0.6 9.7 %collective-permute-start = (s32[1,2]{1,0:T(1,128)}, s32[1,2]{1,0:T(1,128)S(1)}, u32[]{:S(2)}, u32[]{:S(2)}) collective-permute-start(s32[1,2]{1,0:T(1,128)} %mine_ref.1), channel_id=1, source_target_pairs={{0,16},{16,0},{32,48},{48,32},{64,80},{80,64},{96,112},{112,96},{1... | collective-permute-start | bytes 32 | tf_op jit(solution)/shard_map/ppermute | solution.py:147
  10.4 1.6 %copy-start = (f32[256,2048]{1,0:T(8,128)S(1)}, f32[256,2048]{1,0:T(8,128)}, u32[]{:S(2)}) copy-start(f32[256,2048]{1,0:T(8,128)} %colloc_ref.1) | copy-start | bytes 6291460
  11.9 0.7 copy-start.1
  12.6 19.0 %copy-start.3 = (f32[1,8,128,128]{3,2,1,0:T(8,128)S(1)}, f32[1,8,128,128]{3,2,1,0:T(8,128)}, u32[]{:S(2)}) copy-start(f32[1,8,128,128]{3,2,1,0:T(8,128)} %param.6) | copy-start | bytes 1572868
  12.6 42.4 %copy-start.2 = (f32[8,4096]{1,0:T(8,128)S(1)}, f32[8,4096]{1,0:T(8,128)}, u32[]{:S(2)}) copy-start(f32[8,4096]{1,0:T(8,128)} %coef_ref.1) | copy-start | bytes 393220
  26.3 14.5 %collective-permute-start.2 = (f32[512,256]{1,0:T(8,128)S(1)}, f32[512,256]{1,0:T(8,128)S(1)}, u32[]{:S(2)}, u32[]{:S(2)}) collective-permute-start(f32[512,256]{1,0:T(8,128)S(1)} %all_gather.3.own_ref), channel_id=1, source_target_pairs={{0,12},{1,13},{2,14},{3,15},{4,0},{5,1},{6,2},{7,3},{8,4},{9,5},{1... | collective-permute-start | bytes 1572872 | tf_op jit(solution)/shard_map/ppermute | solution.py:163
  29.5 16.2 %collective-permute-start.1 = (f32[512,256]{1,0:T(8,128)S(1)}, f32[512,256]{1,0:T(8,128)S(1)}, u32[]{:S(2)}, u32[]{:S(2)}) collective-permute-start(f32[512,256]{1,0:T(8,128)S(1)} %all_gather.3.own_ref), channel_id=1, source_target_pairs={{0,4},{1,5},{2,6},{3,7},{4,8},{5,9},{6,10},{7,11},{8,12},{9,13},{1... | collective-permute-start | bytes 1572872 | tf_op jit(solution)/shard_map/ppermute | solution.py:162
  31.6 17.9 %collective-permute-start.5 = (f32[1,8,128,128]{3,2,1,0:T(8,128)S(1)}, f32[1,8,128,128]{3,2,1,0:T(8,128)S(1)}, u32[]{:S(2)}, u32[]{:S(2)}) collective-permute-start(f32[1,8,128,128]{3,2,1,0:T(8,128)S(1)} %copy-done.3), channel_id=1, source_target_pairs={{0,0},{16,256},{32,32},{48,288},{64,64},{80,320},{96,96},{112,352}... | collective-permute-start | bytes 1572872 | tf_op jit(solution)/shard_map/ppermute | solution.py:148
  40.8 9.1 %collective-permute-start.4 = (f32[256,256]{1,0:T(8,128)S(1)}, f32[256,256]{1,0:T(8,128)S(1)}, u32[]{:S(2)}, u32[]{:S(2)}) collective-permute-start(f32[256,256]{1,0:T(8,128)S(1)} %slice.9), channel_id=1, source_target_pairs={{0,12},{1,13},{2,14},{3,15},{4,0},{5,1},{6,2},{7,3},{8,4},{9,5},{1... | collective-permute-start | bytes 786440 | tf_op jit(solution)/shard_map/ppermute | solution.py:166
  45.7 9.3 %collective-permute-start.3 = (f32[256,256]{1,0:T(8,128)S(1)}, f32[256,256]{1,0:T(8,128)S(1)}, u32[]{:S(2)}, u32[]{:S(2)}) collective-permute-start(f32[256,256]{1,0:T(8,128)S(1)} %slice.8), channel_id=1, source_target_pairs={{0,4},{1,5},{2,6},{3,7},{4,8},{5,9},{6,10},{7,11},{8,12},{9,13},{1... | collective-permute-start | bytes 786440 | tf_op jit(solution)/shard_map/ppermute | solution.py:165
  57.5 5.9 %collective-permute-start.6 = (f32[8,128,128]{2,1,0:T(8,128)S(1)}, f32[8,128,128]{2,1,0:T(8,128)S(1)}, u32[]{:S(2)}, u32[]{:S(2)}) collective-permute-start(f32[8,128,128]{2,1,0:T(8,128)S(1)} %get-tuple-element.7.u_ref), channel_id=1, source_target_pairs={{0,16},{16,0},{32,48},{48,32},{64,80},{80,64},{96,112},{112,96},{1... | collective-permute-start | bytes 1572872 | tf_op jit(solution)/shard_map/ppermute | solution.py:187
  63.7 28.5 %collective-permute-start.7 = (f32[1,8,128,128]{3,2,1,0:T(8,128)S(1)}, f32[1,8,128,128]{3,2,1,0:T(8,128)S(1)}, u32[]{:S(2)}, u32[]{:S(2)}) collective-permute-start(f32[1,8,128,128]{3,2,1,0:T(8,128)S(1)} %bitcast.2), channel_id=1, source_target_pairs={{0,0},{16,256},{32,32},{48,288},{64,64},{80,320},{96,96},{112,352}... | collective-permute-start | bytes 1572872 | tf_op jit(solution)/shard_map/ppermute | solution.py:197
  73.0 9.2 %collective-permute-start.8 = (f32[8,8,128]{2,1,0:T(8,128)S(1)}, f32[8,8,128]{2,1,0:T(8,128)S(1)}, u32[]{:S(2)}, u32[]{:S(2)}) collective-permute-start(f32[8,8,128]{2,1,0:T(8,128)S(1)} %get-tuple-element.11), channel_id=1, source_target_pairs={{0,32},{16,48},{32,0},{48,16},{64,96},{80,112},{96,64},{112,80},{1... | collective-permute-start | bytes 98312 | tf_op jit(solution)/shard_map/ppermute | solution.py:214

commit v2 on v0

v2 whole, which is shorter than its diff:
```python
import jax
import jax.numpy as jnp
from jax import lax
from jax.experimental import pallas as pl
from jax.experimental.pallas import tpu as pltpu
from jax.sharding import PartitionSpec as P

NX, NZ = 4, 4
NY, NZH, NC = 8, 2, 2
MIRROR = NY * NZH * NC
HALF = MIRROR // 2
bf16, f32 = jnp.bfloat16, jnp.float32
VMEM = pl.BlockSpec(memory_space=pltpu.VMEM)
SMEM = pl.BlockSpec(memory_space=pltpu.SMEM)
ANY = pl.BlockSpec(memory_space=pl.ANY)


def params(mib):
    return pltpu.CompilerParams(vmem_limit_bytes=mib * 1024 * 1024)


def cost(flops, mib):
    return pl.CostEstimate(flops=flops, bytes_accessed=mib << 20, transcendentals=0)


def swap_pairs():
    out = []
    for m in range(MIRROR):
        low = m < HALF
        if low and m % 2 == 1:
            out.append((m, m + HALF - 1))
        elif not low and m % 2 == 0:
            out.append((m, m - HALF + 1))
        else:
            out.append((m, m))
    return out


def x_trade(mask):
    return [(x * NZ + z, (x ^ mask) * NZ + z) for x in range(NX) for z in range(NZ)]


def sources(x):
    return [x, x + 1 - 2 * lax.rem(x, 2), NX - 1 - x, lax.rem(x + 2, NX)]


def split(v):
    hi = v.astype(bf16)
    return hi, (v - hi.astype(f32)).astype(bf16)


def pick_kernel(mine_ref, mate_ref, colloc_ref, out_ref, sems):
    m = lax.axis_index("mirror")
    core = lax.rem(m, 2)
    keeps = core != (m < HALF).astype(jnp.int32)
    p = jnp.where(keeps, mine_ref[0, 0], mate_ref[0, 1])
    q = jnp.where(keeps, mine_ref[0, 1], mate_ref[0, 0])
    n = out_ref.shape[0]
    row = pl.multiple_of(core * n, n)
    copies = []
    for k, block in enumerate((p, q)):
        copies.append(
            pltpu.make_async_copy(
                colloc_ref.at[pl.ds(row, n), pl.ds(pl.multiple_of(block * 128, 128), 128)],
                out_ref.at[:, pl.ds(k * 128, 128)],
                sems.at[k],
            )
        )
    for c in copies:
        c.start()
    for c in copies:
        c.wait()


def fit_part(coef_ref, rows, xs, lt_ref, rt_ref, n, whi, wlo):
    core = lax.rem(lax.axis_index("mirror"), 2)
    left, right = rows[:, :128], rows[:, 128:]
    lt, rt = left.T, right.T
    cols = pl.ds(n * 512, 512)
    lt_ref[:, cols] = lt
    rhi, rlo = split(right)
    rthi, rtlo = split(rt)
    rt_ref[0:128, cols] = rthi
    rt_ref[128:256, cols] = rtlo
    both = jnp.concatenate([rhi, rlo], axis=1)
    cs = []
    for z in range(NZ):
        at = pl.multiple_of((xs * NZ + z) * 256 + core * 128, 128)
        cs.append(coef_ref[:, pl.ds(at, 128)])
    cf = jnp.concatenate(cs, axis=1)
    for a in range(coef_ref.shape[0]):
        hi, lo = split(cf[a : a + 1, :] * lt)
        whi[pl.ds(a * 128, 128), :] = hi
        wlo[pl.ds(a * 128, 128), :] = lo
    part = jnp.dot(whi[...], both, preferred_element_type=f32)
    return part + jnp.dot(wlo[...], both, preferred_element_type=f32)


def fit_first_kernel(own, near0, near1, side0, side1, coef_ref, acc_ref, lt_ref, rt_ref, whi, wlo):
    xs = sources(lax.axis_index("blk") // NZ)
    for n, refs in enumerate(((own,), (near0, near1), (side0, side1))):
        rows = jnp.concatenate([r[...] for r in refs], axis=0)
        part = fit_part(coef_ref, rows, xs[n], lt_ref, rt_ref, n, whi, wlo)
        if n == 0:
            acc_ref[...] = part
        else:
            acc_ref[...] += part


def fit_last_kernel(far0, far1, acc_ref, coef_ref, t_ref, u_ref, lt_ref, rt_ref, whi, wlo):
    xs = sources(lax.axis_index("blk") // NZ)
    rows = jnp.concatenate([far0[...], far1[...]], axis=0)
    tot = acc_ref[...] + fit_part(coef_ref, rows, xs[3], lt_ref, rt_ref, 0, whi, wlo)
    fit = tot[:, :128] + tot[:, 128:]
    u_ref[...] = 0.5 * t_ref[...] - fit.reshape(t_ref.shape)


def blocks(parity, lt_refs, rt_refs, out_ref, hh, ll):
    for n, xs in enumerate(sources(lax.axis_index("blk") // NZ)):
        lt_ref, rt_ref = (lt_refs[0], rt_refs[0]) if n < 3 else (lt_refs[1], rt_refs[1])
        at = n * 512 if n < 3 else 0
        cols = [pl.ds(pl.multiple_of(at + j * 256 + parity * 128, 128), 128) for j in range(2)]
        rt = jnp.concatenate([rt_ref[:, c] for c in cols], axis=1)
        lt = jnp.concatenate([lt_ref[:, c] for c in cols], axis=1)
        spread = jnp.dot(hh[...], rt, preferred_element_type=f32)
        spread += jnp.dot(ll[...], rt, preferred_element_type=f32)
        terms = []
        for a in range(out_ref.shape[1]):
            terms.append(jnp.sum(spread[a * 128 : (a + 1) * 128] * lt, axis=0, keepdims=True))
        block = jnp.concatenate(terms, axis=0)
        for j in range(2):
            out_ref[xs * 2 + j] = block[:, j * 128 : (j + 1) * 128]


def send_kernel(u_ref, o_ref, lt0, lt1, rt0, rt1, out_ref, hh_ref, ll_ref, r_ref):
    zh = lax.rem(lax.axis_index("mirror") // NC, NZH)
    for a in range(u_ref.shape[0]):
        r = u_ref[a] + o_ref[a].T
        r_ref[a] = r
        hi, lo = split(2.0 * r)
        rows = pl.ds(a * 128, 128)
        hh_ref[rows, 0:128] = hi
        hh_ref[rows, 128:256] = hi
        ll_ref[rows, 0:128] = lo
        ll_ref[rows, 128:256] = lo
    blocks(1 - zh, (lt0, lt1), (rt0, rt1), out_ref, hh_ref, ll_ref)


def keep_kernel(lt0, lt1, rt0, rt1, hh_ref, ll_ref, out_ref):
    zh = lax.rem(lax.axis_index("mirror") // NC, NZH)
    blocks(zh, (lt0, lt1), (rt0, rt1), out_ref, hh_ref, ll_ref)


def per_device(colloc, coeffs, targets, pair_list):
    naux, nb = targets.shape[1], targets.shape[2]
    shape = jax.ShapeDtypeStruct
    mates = [(m, m ^ 1) for m in range(MIRROR)]
    mate = lax.ppermute(pair_list, "mirror", mates)
    work = lax.ppermute(targets, "mirror", swap_pairs())[0]
    rows = pl.pallas_call(
        pick_kernel,
        out_shape=shape((colloc.shape[0] // 2, 2 * nb), f32),
        in_specs=[SMEM, SMEM, ANY],
        out_specs=VMEM,
        scratch_shapes=[pltpu.SemaphoreType.DMA((2,))],
        compiler_params=params(8),
        name="pick",
    )(pair_list, mate, colloc)

    z_groups = [[x * NZ + z for z in range(NZ)] for x in range(NX)]
    own = lax.all_gather(rows, "blk", axis=0, tiled=True, axis_index_groups=z_groups)
    h = own.shape[0] // 2
    side0 = lax.ppermute(own[:h], "blk", x_trade(3))
    near1 = lax.ppermute(own[h:], "blk", x_trade(1))
    side1 = lax.ppermute(own[h:], "blk", x_trade(3))
    near0 = lax.ppermute(own[:h], "blk", x_trade(1))
    far1 = lax.ppermute(near1, "blk", x_trade(3))
    far0 = lax.ppermute(side0, "blk", x_trade(1))

    unit = 2 * 1024 * 2048 * 128
    weights = [pltpu.VMEM((naux * nb, 512), bf16)] * 2
    acc, lt0, rt0 = pl.pallas_call(
        fit_first_kernel,
        out_shape=(shape((naux * nb, 2 * nb), f32), shape((nb, 1536), f32), shape((2 * nb, 1536), bf16)),
        in_specs=[VMEM] * 6,
        out_specs=[VMEM] * 3,
        scratch_shapes=weights,
        compiler_params=params(16),
        cost_estimate=cost(3 * unit, 5),
        name="fit_first",
    )(own, near0, near1, side0, side1, coeffs)
    u, lt1, rt1 = pl.pallas_call(
        fit_last_kernel,
        out_shape=(shape((naux, nb, nb), f32), shape((nb, 512), f32), shape((2 * nb, 512), bf16)),
        in_specs=[VMEM] * 5,
        out_specs=[VMEM] * 3,
        scratch_shapes=weights,
        compiler_params=params(16),
        cost_estimate=cost(unit, 3),
        name="fit_last",
    )(far0, far1, acc, coeffs, work)

    other = lax.ppermute(u, "mirror", mates)
    half = shape((NY, naux, nb), f32)
    stacked = shape((naux * nb, 2 * nb), bf16)
    send, hh, ll, res = pl.pallas_call(
        send_kernel,
        out_shape=(half, stacked, stacked, shape((naux, nb, nb), f32)),
        in_specs=[VMEM] * 6,
        out_specs=[VMEM] * 4,
        compiler_params=params(16),
        cost_estimate=cost(2 * unit, 4),
        name="gradient_send",
    )(u, other, lt0, lt1, rt0, rt1)
    residual = lax.ppermute(res[None], "mirror", swap_pairs())
    moved = lax.ppermute(send, "mirror", [(m, m ^ NC) for m in range(MIRROR)])
    keep = pl.pallas_call(
        keep_kernel,
        out_shape=half,
        in_specs=[VMEM] * 6,
        out_specs=VMEM,
        compiler_params=params(16),
        cost_estimate=cost(2 * unit, 4),
        name="gradient_keep",
    )(lt0, lt1, rt0, rt1, hh, ll)
    y_groups = [[(y * NZH + h) * NC + c for y in range(NY)] for h in range(NZH) for c in range(NC)]
    spread = lax.all_to_all(keep + moved, "mirror", 0, 0, tiled=True, axis_index_groups=y_groups)
    return residual, jnp.sum(spread, axis=0)


def solution(mesh):
    return jax.shard_map(
        per_device,
        mesh=mesh,
        in_specs=(
            P("blk", None),
            P("blk", None),
            P("mirror", "blk", None, None),
            P("mirror", None),
        ),
        out_specs=(P("mirror", "blk", None, None), P("blk", "mirror")),
        check_vma=False,
    )
```

time: 310 us -> 88.9 us (0.29); the launches traced: 304 us -> 87.5 us
  waiting for transfers between devices: 213 us -> 8.21 us
  starting transfers between devices: 8.36 us -> 41.8 us
  local copies, waits for them, and re-layouts: 34 us -> 3.07 us
  matrix products: 30.8 us -> 0 us
  blocking collectives: 0 us -> 27.1 us
  between operations: 15.3 us -> 0.81 us
  Pallas kernels: 0 us -> 5.88 us
    reduce_scatter x1 -> x0, waiting for transfers between devices: 112 us -> none  [per_device(): lax.psum_scatter(grid_terms, 'mirror', scatter_dimension=1, tiled=True)]
    all_gather x1 -> x0, waiting for transfers between devices: 101 us -> none  [per_device(): gathered = lax.all_gather(paired, 'blk', axis=0, tiled=True)]
    ppermute x1 -> x11, starting transfers between devices: 8.28 us -> 41.8 us  [the longest x1 8.79 us: per_device(): mate = lax.ppermute(pair_list, 'mirror', mates)]
    squeeze x16 -> x0, local copies, waits for them, and re-layouts: 17.3 us -> none  [fold_project(): lax.scan(step_fn, running_sum, (stacked_coef, stacked_rows))]
    all_gather x0 -> x1, blocking collectives: none -> 17.2 us  [per_device(): lax.all_gather(rows, 'blk', axis=0, tiled=True, axis_index_groups=z_groups)]
    dot_general x8 -> x0, matrix products: 15.8 us -> none  [project_rows(): jnp.einsum('agp,gq->apq', weighted, row_block[:, block_width:], precision...]
    while x8 -> x0, matrix products: 14.9 us -> none
    all_to_all x0 -> x1, blocking collectives: none -> 9.92 us  [per_device(): lax.all_to_all(keep + moved, 'mirror', 0, 0, tiled=True, axis_index_group...]
  transfers between devices with their start and end apart: 3 -> 11, of which waited for: 2 -> 5; matrix products, arithmetic and copies ran while one was open for 11% -> 1% of each run, Pallas kernels for 0% -> 4%
where the time goes in v2:
time: 88.9 us; the launch traced here: 87.5 us
  starting transfers between devices  41.8 us (47%)
  blocking collectives  27.1 us (30%)
  waiting for transfers between devices  8.21 us (9%)
  Pallas kernels  5.88 us (7%)
  local copies, waits for them, and re-layouts  3.07 us (3%)
    all_gather x1, blocking collectives, per_device(): lax.all_gather(rows, 'blk', axis=0, tiled=True, axis_index_groups=z_groups)  17.2 us
    all_to_all x1, blocking collectives, per_device(): lax.all_to_all(keep + moved, 'mirror', 0, 0, tiled=True, axis_index_group...  9.92 us
    ppermute x1, starting transfers between devices, per_device(): mate = lax.ppermute(pair_list, 'mirror', mates)  8.79 us
    ppermute x1, starting transfers between devices, per_device(): moved = lax.ppermute(send, 'mirror', [(m, m ^ NC) for m in range(MIRROR)])  6.84 us
    ppermute x1, starting transfers between devices, per_device(): residual = lax.ppermute(res[None], 'mirror', swap_pairs())  4.91 us
    ppermute x1, starting transfers between devices, per_device(): near0 = lax.ppermute(own[:h], 'blk', x_trade(1))  3.36 us
    ppermute x1, starting transfers between devices, per_device(): side1 = lax.ppermute(own[h:], 'blk', x_trade(3))  3.32 us
    ppermute x1, starting transfers between devices, per_device(): side0 = lax.ppermute(own[:h], 'blk', x_trade(3))  3.17 us
  transfers between devices with their start and end apart: 11, of which 5 were waited for; matrix products, arithmetic and copies ran while one was open for 1% of the time, Pallas kernels for 4%

profile of v2, /device:TPU:1, one launch (start us, length us, event | category | flops | bytes accessed | tf_op | source)
XLA Modules:
  0.0 87.5 jit_solution(15874686518866539464)
XLA Ops:
  0.6 8.8 %collective-permute-start = (s32[1,2]{1,0:T(1,128)}, s32[1,2]{1,0:T(1,128)S(1)}, u32[]{:S(2)}, u32[]{:S(2)}) collective-permute-start(s32[1,2]{1,0:T(1,128)} %mine_ref.1), channel_id=1, source_target_pairs={{0,16},{16,0},{32,48},{48,32},{64,80},{80,64},{96,112},{112,96},{1... | collective-permute-start | bytes 32 | tf_op jit(solution)/shard_map/ppermute | solution.py:158
  9.4 2.0 %collective-permute-start.7 = (f32[1,8,128,128]{3,2,1,0:T(8,128)}, f32[1,8,128,128]{3,2,1,0:T(8,128)S(1)}, u32[]{:S(2)}, u32[]{:S(2)}) collective-permute-start(f32[1,8,128,128]{3,2,1,0:T(8,128)} %param.6), channel_id=1, source_target_pairs={{0,0},{16,256},{32,32},{48,288},{64,64},{80,320},{96,96},{112,352}... | collective-permute-start | bytes 1572872 | tf_op jit(solution)/shard_map/ppermute | solution.py:159
  11.4 1.6 %copy-done = f32[256,2048]{1,0:T(8,128)S(1)} copy-done((f32[256,2048]{1,0:T(8,128)S(1)}, f32[256,2048]{1,0:T(8,128)}, u32[]{:S(2)}) %copy-start) | copy-done | bytes 2097176
  13.0 0.7 copy-done.2
  14.3 17.2 %all_gather.3.own = f32[512,256]{1,0:T(8,128)S(1)} all-gather(f32[128,256]{1,0:T(8,128)S(1)} %pick.1), channel_id=1, replica_groups={{0,1,2,3},{4,5,6,7},{8,9,10,11},{12,13,14,15},{16,17,18,19},{20,21,22,2..., dimensions={0}, use_global_device_ids=true | all-gather | bytes 655360 | tf_op jit(solution)/shard_map/all_gather | solution.py:171
  31.5 3.2 %collective-permute-start.1 = (f32[256,256]{1,0:T(8,128)S(1)}, f32[256,256]{1,0:T(8,128)S(1)}, u32[]{:S(2)}, u32[]{:S(2)}) collective-permute-start(f32[256,256]{1,0:T(8,128)S(1)} %get-tuple-element.23), channel_id=1, source_target_pairs={{0,12},{1,13},{2,14},{3,15},{4,8},{5,9},{6,10},{7,11},{8,4},{9,5},... | collective-permute-start | bytes 786440 | tf_op jit(solution)/shard_map/ppermute | solution.py:173
  34.7 1.9 %collective-permute-start.3 = (f32[256,256]{1,0:T(8,128)S(1)}, f32[256,256]{1,0:T(8,128)S(1)}, u32[]{:S(2)}, u32[]{:S(2)}) collective-permute-start(f32[256,256]{1,0:T(8,128)S(1)} %get-tuple-element.22), channel_id=1, source_target_pairs={{0,4},{1,5},{2,6},{3,7},{4,0},{5,1},{6,2},{7,3},{8,12},{9,13},{10,... | collective-permute-start | bytes 786440 | tf_op jit(solution)/shard_map/ppermute | solution.py:174
  36.6 3.4 %collective-permute-start.5 = (f32[256,256]{1,0:T(8,128)S(1)}, f32[256,256]{1,0:T(8,128)S(1)}, u32[]{:S(2)}, u32[]{:S(2)}) collective-permute-start(f32[256,256]{1,0:T(8,128)S(1)} %get-tuple-element.23), channel_id=1, source_target_pairs={{0,4},{1,5},{2,6},{3,7},{4,0},{5,1},{6,2},{7,3},{8,12},{9,13},{10,... | collective-permute-start | bytes 786440 | tf_op jit(solution)/shard_map/ppermute | solution.py:176
  40.0 3.3 %collective-permute-start.6 = (f32[256,256]{1,0:T(8,128)S(1)}, f32[256,256]{1,0:T(8,128)S(1)}, u32[]{:S(2)}, u32[]{:S(2)}) collective-permute-start(f32[256,256]{1,0:T(8,128)S(1)} %get-tuple-element.22), channel_id=1, source_target_pairs={{0,12},{1,13},{2,14},{3,15},{4,8},{5,9},{6,10},{7,11},{8,4},{9,5},... | collective-permute-start | bytes 786440 | tf_op jit(solution)/shard_map/ppermute | solution.py:175
  43.3 1.9 %collective-permute-start.2 = (f32[256,256]{1,0:T(8,128)S(1)}, f32[256,256]{1,0:T(8,128)S(1)}, u32[]{:S(2)}, u32[]{:S(2)}) collective-permute-start(f32[256,256]{1,0:T(8,128)S(1)} %collective-permute-done.1.side0), channel_id=1, source_target_pairs={{0,4},{1,5},{2,6},{3,7},{4,0},{5,1},{6,2},{7,3},{8,12},{9,13},{10,... | collective-permute-start | bytes 786440 | tf_op jit(solution)/shard_map/ppermute | solution.py:178
  45.3 3.2 %collective-permute-start.4 = (f32[256,256]{1,0:T(8,128)S(1)}, f32[256,256]{1,0:T(8,128)S(1)}, u32[]{:S(2)}, u32[]{:S(2)}) collective-permute-start(f32[256,256]{1,0:T(8,128)S(1)} %collective-permute-done.3.near1), channel_id=1, source_target_pairs={{0,12},{1,13},{2,14},{3,15},{4,8},{5,9},{6,10},{7,11},{8,4},{9,5},... | collective-permute-start | bytes 786440 | tf_op jit(solution)/shard_map/ppermute | solution.py:177
  48.5 1.0 %collective-permute-done.6.side1 = f32[256,256]{1,0:T(8,128)S(1)} collective-permute-done((f32[256,256]{1,0:T(8,128)S(1)}, f32[256,256]{1,0:T(8,128)S(1)}, u32[]{:S(2)}, u32[]{:S(2)}) %collective-permute-start.6) | collective-permute-done | bytes 262176 | tf_op jit(solution)/shard_map/ppermute | solution.py:175
  49.4 1.9 %fit_first.1 = (f32[1024,256]{1,0:T(8,128)S(1)}, f32[128,1536]{1,0:T(8,128)S(1)}, bf16[256,1536]{1,0:T(8,128)(2,1)S(1)}) custom-call(f32[512,256]{1,0:T(8,128)S(1)} %all_gather.3.own, f32[256,256]{1,0:T(8,128)S(1)} %collective-permute-done.5.near0, f32[256,256]{1,0:T(8,128)S(1)} %collective-permute-done.3.near1, ...), custom_call_target="tpu_custom_call" | custom-call | flops 1610612736 | bytes 5242880 | tf_op jit(solution)/shard_map/fit_first/pallas_call | solution.py:182
  51.3 2.6 %collective-permute-done.2.far0 = f32[256,256]{1,0:T(8,128)S(1)} collective-permute-done((f32[256,256]{1,0:T(8,128)S(1)}, f32[256,256]{1,0:T(8,128)S(1)}, u32[]{:S(2)}, u32[]{:S(2)}) %collective-permute-start.2) | collective-permute-done | bytes 262176 | tf_op jit(solution)/shard_map/ppermute | solution.py:178
  53.9 2.7 %collective-permute-done.4.far1 = f32[256,256]{1,0:T(8,128)S(1)} collective-permute-done((f32[256,256]{1,0:T(8,128)S(1)}, f32[256,256]{1,0:T(8,128)S(1)}, u32[]{:S(2)}, u32[]{:S(2)}) %collective-permute-start.4) | collective-permute-done | bytes 262176 | tf_op jit(solution)/shard_map/ppermute | solution.py:177
  56.6 0.8 fit_last.1
  57.4 2.4 %collective-permute-start.8 = (f32[8,128,128]{2,1,0:T(8,128)S(1)}, f32[8,128,128]{2,1,0:T(8,128)S(1)}, u32[]{:S(2)}, u32[]{:S(2)}) collective-permute-start(f32[8,128,128]{2,1,0:T(8,128)S(1)} %get-tuple-element.13.u_ref), channel_id=1, source_target_pairs={{0,16},{16,0},{32,48},{48,32},{64,80},{80,64},{96,112},{112,96},{1... | collective-permute-start | bytes 1572872 | tf_op jit(solution)/shard_map/ppermute | solution.py:203
  59.8 1.5 %collective-permute-done.8.o_ref = f32[8,128,128]{2,1,0:T(8,128)S(1)} collective-permute-done((f32[8,128,128]{2,1,0:T(8,128)S(1)}, f32[8,128,128]{2,1,0:T(8,128)S(1)}, u32[]{:S(2)}, u32[]{:S(2)}) %collective-permute-start.8) | collective-permute-done | bytes 524320 | tf_op jit(solution)/shard_map/ppermute | solution.py:203
  61.3 1.4 %gradient_send.1 = (f32[8,8,128]{2,1,0:T(8,128)S(1)}, bf16[1024,256]{1,0:T(8,128)(2,1)S(1)}, bf16[1024,256]{1,0:T(8,128)(2,1)S(1)}, f32[8,128,128]{2,1,0:T(8,128)S(1)}) custom-call(f32[8,128,128]{2,1,0:T(8,128)S(1)} %get-tuple-element.13.u_ref, f32[8,128,128]{2,1,0:T(8,128)S(1)} %collective-permute-done.8.o_ref, f32[128,1536]{1,0:T(8,128)S(1)} %get-tuple-element.14.lt0, ...), custom_call_target="tpu_custom_call" | custom-call | flops 1073741824 | bytes 4194304 | tf_op jit(solution)/shard_map/gradient_send/pallas_call | solution.py:206
  62.7 4.9 %collective-permute-start.9 = (f32[1,8,128,128]{3,2,1,0:T(8,128)S(1)}, f32[1,8,128,128]{3,2,1,0:T(8,128)S(1)}, u32[]{:S(2)}, u32[]{:S(2)}) collective-permute-start(f32[1,8,128,128]{3,2,1,0:T(8,128)S(1)} %bitcast.3), channel_id=1, source_target_pairs={{0,0},{16,256},{32,32},{48,288},{64,64},{80,320},{96,96},{112,352}... | collective-permute-start | bytes 1572872 | tf_op jit(solution)/shard_map/ppermute | solution.py:215
  67.6 6.8 %collective-permute-start.10 = (f32[8,8,128]{2,1,0:T(8,128)S(1)}, f32[8,8,128]{2,1,0:T(8,128)S(1)}, u32[]{:S(2)}, u32[]{:S(2)}) collective-permute-start(f32[8,8,128]{2,1,0:T(8,128)S(1)} %get-tuple-element.21), channel_id=1, source_target_pairs={{0,32},{16,48},{32,0},{48,16},{64,96},{80,112},{96,64},{112,80},{1... | collective-permute-start | bytes 98312 | tf_op jit(solution)/shard_map/ppermute | solution.py:216
  74.4 1.3 %gradient_keep.1 = f32[8,8,128]{2,1,0:T(8,128)S(1)} custom-call(f32[128,1536]{1,0:T(8,128)S(1)} %get-tuple-element.14.lt0, f32[128,512]{1,0:T(8,128)S(1)} %get-tuple-element.15.lt1, bf16[256,1536]{1,0:T(8,128)(2,1)S(1)} %get-tuple-element.16.rt0, bf16[256,512]{1,0:T(8,128)(2,1)S(1)} %get-tuple-element.17.rt1, ...), custom_call_target="tpu_custom_call" | custom-call | flops 1073741824 | bytes 4194304 | tf_op jit(solution)/shard_map/gradient_keep/pallas_call | solution.py:217
  76.1 9.9 %all_to_all.5 = f32[8,8,128]{2,1,0:T(8,128)S(1)} all-to-all(f32[8,8,128]{2,1,0:T(8,128)S(1)} %add.3), channel_id=1, replica_groups={{0,64,128,192,256,320,384,448},{16,80,144,208,272,336,400,464},{32,96,1..., dimensions={0} | all-to-all | bytes 65536 | tf_op jit(solution)/shard_map/all_to_all | solution.py:227
  86.7 0.8 copy.7
  (15 shorter events, 1.7 us)
Async XLA Ops:
  0.6 10.8 %collective-permute-start = (s32[1,2]{1,0:T(1,128)}, s32[1,2]{1,0:T(1,128)S(1)}, u32[]{:S(2)}, u32[]{:S(2)}) collective-permute-start(s32[1,2]{1,0:T(1,128)} %mine_ref.1), channel_id=1, source_target_pairs={{0,16},{16,0},{32,48},{48,32},{64,80},{80,64},{96,112},{112,96},{1... | collective-permute-start | bytes 32 | tf_op jit(solution)/shard_map/ppermute | solution.py:158
  9.4 41.9 %collective-permute-start.7 = (f32[1,8,128,128]{3,2,1,0:T(8,128)}, f32[1,8,128,128]{3,2,1,0:T(8,128)S(1)}, u32[]{:S(2)}, u32[]{:S(2)}) collective-permute-start(f32[1,8,128,128]{3,2,1,0:T(8,128)} %param.6), channel_id=1, source_target_pairs={{0,0},{16,256},{32,32},{48,288},{64,64},{80,320},{96,96},{112,352}... | collective-permute-start | bytes 1572872 | tf_op jit(solution)/shard_map/ppermute | solution.py:159
  11.4 1.6 %copy-start = (f32[256,2048]{1,0:T(8,128)S(1)}, f32[256,2048]{1,0:T(8,128)}, u32[]{:S(2)}) copy-start(f32[256,2048]{1,0:T(8,128)} %colloc_ref.1) | copy-start | bytes 6291460
  13.0 0.7 copy-start.2
  13.7 35.8 %copy-start.1 = (f32[8,4096]{1,0:T(8,128)S(1)}, f32[8,4096]{1,0:T(8,128)}, u32[]{:S(2)}) copy-start(f32[8,4096]{1,0:T(8,128)} %coef_ref.3) | copy-start | bytes 393220
  31.5 11.8 %collective-permute-start.1 = (f32[256,256]{1,0:T(8,128)S(1)}, f32[256,256]{1,0:T(8,128)S(1)}, u32[]{:S(2)}, u32[]{:S(2)}) collective-permute-start(f32[256,256]{1,0:T(8,128)S(1)} %get-tuple-element.23), channel_id=1, source_target_pairs={{0,12},{1,13},{2,14},{3,15},{4,8},{5,9},{6,10},{7,11},{8,4},{9,5},... | collective-permute-start | bytes 786440 | tf_op jit(solution)/shard_map/ppermute | solution.py:173
  34.7 10.6 %collective-permute-start.3 = (f32[256,256]{1,0:T(8,128)S(1)}, f32[256,256]{1,0:T(8,128)S(1)}, u32[]{:S(2)}, u32[]{:S(2)}) collective-permute-start(f32[256,256]{1,0:T(8,128)S(1)} %get-tuple-element.22), channel_id=1, source_target_pairs={{0,4},{1,5},{2,6},{3,7},{4,0},{5,1},{6,2},{7,3},{8,12},{9,13},{10,... | collective-permute-start | bytes 786440 | tf_op jit(solution)/shard_map/ppermute | solution.py:174
  36.6 11.8 %collective-permute-start.5 = (f32[256,256]{1,0:T(8,128)S(1)}, f32[256,256]{1,0:T(8,128)S(1)}, u32[]{:S(2)}, u32[]{:S(2)}) collective-permute-start(f32[256,256]{1,0:T(8,128)S(1)} %get-tuple-element.23), channel_id=1, source_target_pairs={{0,4},{1,5},{2,6},{3,7},{4,0},{5,1},{6,2},{7,3},{8,12},{9,13},{10,... | collective-permute-start | bytes 786440 | tf_op jit(solution)/shard_map/ppermute | solution.py:176
  40.0 9.4 %collective-permute-start.6 = (f32[256,256]{1,0:T(8,128)S(1)}, f32[256,256]{1,0:T(8,128)S(1)}, u32[]{:S(2)}, u32[]{:S(2)}) collective-permute-start(f32[256,256]{1,0:T(8,128)S(1)} %get-tuple-element.22), channel_id=1, source_target_pairs={{0,12},{1,13},{2,14},{3,15},{4,8},{5,9},{6,10},{7,11},{8,4},{9,5},... | collective-permute-start | bytes 786440 | tf_op jit(solution)/shard_map/ppermute | solution.py:175
  43.3 10.5 %collective-permute-start.2 = (f32[256,256]{1,0:T(8,128)S(1)}, f32[256,256]{1,0:T(8,128)S(1)}, u32[]{:S(2)}, u32[]{:S(2)}) collective-permute-start(f32[256,256]{1,0:T(8,128)S(1)} %collective-permute-done.1.side0), channel_id=1, source_target_pairs={{0,4},{1,5},{2,6},{3,7},{4,0},{5,1},{6,2},{7,3},{8,12},{9,13},{10,... | collective-permute-start | bytes 786440 | tf_op jit(solution)/shard_map/ppermute | solution.py:178
  45.3 11.3 %collective-permute-start.4 = (f32[256,256]{1,0:T(8,128)S(1)}, f32[256,256]{1,0:T(8,128)S(1)}, u32[]{:S(2)}, u32[]{:S(2)}) collective-permute-start(f32[256,256]{1,0:T(8,128)S(1)} %collective-permute-done.3.near1), channel_id=1, source_target_pairs={{0,12},{1,13},{2,14},{3,15},{4,8},{5,9},{6,10},{7,11},{8,4},{9,5},... | collective-permute-start | bytes 786440 | tf_op jit(solution)/shard_map/ppermute | solution.py:177
  57.4 3.9 %collective-permute-start.8 = (f32[8,128,128]{2,1,0:T(8,128)S(1)}, f32[8,128,128]{2,1,0:T(8,128)S(1)}, u32[]{:S(2)}, u32[]{:S(2)}) collective-permute-start(f32[8,128,128]{2,1,0:T(8,128)S(1)} %get-tuple-element.13.u_ref), channel_id=1, source_target_pairs={{0,16},{16,0},{32,48},{48,32},{64,80},{80,64},{96,112},{112,96},{1... | collective-permute-start | bytes 1572872 | tf_op jit(solution)/shard_map/ppermute | solution.py:203
  62.7 24.0 %collective-permute-start.9 = (f32[1,8,128,128]{3,2,1,0:T(8,128)S(1)}, f32[1,8,128,128]{3,2,1,0:T(8,128)S(1)}, u32[]{:S(2)}, u32[]{:S(2)}) collective-permute-start(f32[1,8,128,128]{3,2,1,0:T(8,128)S(1)} %bitcast.3), channel_id=1, source_target_pairs={{0,0},{16,256},{32,32},{48,288},{64,64},{80,320},{96,96},{112,352}... | collective-permute-start | bytes 1572872 | tf_op jit(solution)/shard_map/ppermute | solution.py:215
  67.6 8.6 %collective-permute-start.10 = (f32[8,8,128]{2,1,0:T(8,128)S(1)}, f32[8,8,128]{2,1,0:T(8,128)S(1)}, u32[]{:S(2)}, u32[]{:S(2)}) collective-permute-start(f32[8,8,128]{2,1,0:T(8,128)S(1)} %get-tuple-element.21), channel_id=1, source_target_pairs={{0,32},{16,48},{32,0},{48,16},{64,96},{80,112},{96,64},{112,80},{1... | collective-permute-start | bytes 98312 | tf_op jit(solution)/shard_map/ppermute | solution.py:216

commit v3 on v2

--- a/solution.py
+++ b/solution.py
@@ -12,7 +12,6 @@
 bf16, f32 = jnp.bfloat16, jnp.float32
 VMEM = pl.BlockSpec(memory_space=pltpu.VMEM)
 SMEM = pl.BlockSpec(memory_space=pltpu.SMEM)
-ANY = pl.BlockSpec(memory_space=pl.ANY)
 
 
 def params(mib):
@@ -40,6 +39,15 @@
     return [(x * NZ + z, (x ^ mask) * NZ + z) for x in range(NX) for z in range(NZ)]
 
 
+def z_trade(mask):
+    return [(x * NZ + z, x * NZ + (z ^ mask)) for x in range(NX) for z in range(NZ)]
+
+
+def z_order(z):
+    near = z + 1 - 2 * lax.rem(z, 2)
+    return [z, near, lax.rem(z + 2, NZ), lax.rem(near + 2, NZ)]
+
+
 def sources(x):
     return [x, x + 1 - 2 * lax.rem(x, 2), NX - 1 - x, lax.rem(x + 2, NX)]
 
@@ -49,27 +57,13 @@
     return hi, (v - hi.astype(f32)).astype(bf16)
 
 
-def pick_kernel(mine_ref, mate_ref, colloc_ref, out_ref, sems):
+def pick_kernel(mine_ref, mate_ref, half_ref, out_ref):
     m = lax.axis_index("mirror")
-    core = lax.rem(m, 2)
-    keeps = core != (m < HALF).astype(jnp.int32)
-    p = jnp.where(keeps, mine_ref[0, 0], mate_ref[0, 1])
-    q = jnp.where(keeps, mine_ref[0, 1], mate_ref[0, 0])
-    n = out_ref.shape[0]
-    row = pl.multiple_of(core * n, n)
-    copies = []
+    keeps = lax.rem(m, 2) != (m < HALF).astype(jnp.int32)
+    q = jnp.where(keeps, mine_ref[0, 0], mate_ref[0, 0])
+    p = jnp.where(keeps, mine_ref[0, 1], mate_ref[0, 1])
     for k, block in enumerate((p, q)):
-        copies.append(
-            pltpu.make_async_copy(
-                colloc_ref.at[pl.ds(row, n), pl.ds(pl.multiple_of(block * 128, 128), 128)],
-                out_ref.at[:, pl.ds(k * 128, 128)],
-                sems.at[k],
-            )
-        )
-    for c in copies:
-        c.start()
-    for c in copies:
-        c.wait()
+        out_ref[:, k * 128 : (k + 1) * 128] = half_ref[:, pl.ds(pl.multiple_of(block * 128, 128), 128)]
 
 
 def fit_part(coef_ref, rows, xs, lt_ref, rt_ref, n, whi, wlo):
@@ -84,7 +78,7 @@
     rt_ref[128:256, cols] = rtlo
     both = jnp.concatenate([rhi, rlo], axis=1)
     cs = []
-    for z in range(NZ):
+    for z in z_order(lax.rem(lax.axis_index("blk"), NZ)):
         at = pl.multiple_of((xs * NZ + z) * 256 + core * 128, 128)
         cs.append(coef_ref[:, pl.ds(at, 128)])
     cf = jnp.concatenate(cs, axis=1)
@@ -96,9 +90,9 @@
     return part + jnp.dot(wlo[...], both, preferred_element_type=f32)
 
 
-def fit_first_kernel(own, near0, near1, side0, side1, coef_ref, acc_ref, lt_ref, rt_ref, whi, wlo):
+def fit_first_kernel(own0, own1, own2, own3, near0, near1, side0, side1, coef_ref, acc_ref, lt_ref, rt_ref, whi, wlo):
     xs = sources(lax.axis_index("blk") // NZ)
-    for n, refs in enumerate(((own,), (near0, near1), (side0, side1))):
+    for n, refs in enumerate(((own0, own1, own2, own3), (near0, near1), (side0, side1))):
         rows = jnp.concatenate([r[...] for r in refs], axis=0)
         part = fit_part(coef_ref, rows, xs[n], lt_ref, rt_ref, n, whi, wlo)
         if n == 0:
@@ -116,10 +110,12 @@
 
 
 def blocks(parity, lt_refs, rt_refs, out_ref, hh, ll):
+    z = lax.rem(lax.axis_index("blk"), NZ)
+    first, pair = lax.rem(z + parity, 2), z // 2
     for n, xs in enumerate(sources(lax.axis_index("blk") // NZ)):
         lt_ref, rt_ref = (lt_refs[0], rt_refs[0]) if n < 3 else (lt_refs[1], rt_refs[1])
         at = n * 512 if n < 3 else 0
-        cols = [pl.ds(pl.multiple_of(at + j * 256 + parity * 128, 128), 128) for j in range(2)]
+        cols = [pl.ds(pl.multiple_of(at + j * 256 + first * 128, 128), 128) for j in range(2)]
         rt = jnp.concatenate([rt_ref[:, c] for c in cols], axis=1)
         lt = jnp.concatenate([lt_ref[:, c] for c in cols], axis=1)
         spread = jnp.dot(hh[...], rt, preferred_element_type=f32)
@@ -129,7 +125,7 @@
             terms.append(jnp.sum(spread[a * 128 : (a + 1) * 128] * lt, axis=0, keepdims=True))
         block = jnp.concatenate(terms, axis=0)
         for j in range(2):
-            out_ref[xs * 2 + j] = block[:, j * 128 : (j + 1) * 128]
+            out_ref[xs * 2 + (pair if j == 0 else 1 - pair)] = block[:, j * 128 : (j + 1) * 128]
 
 
 def send_kernel(u_ref, o_ref, lt0, lt1, rt0, rt1, out_ref, hh_ref, ll_ref, r_ref):
@@ -157,38 +153,42 @@
     mates = [(m, m ^ 1) for m in range(MIRROR)]
     mate = lax.ppermute(pair_list, "mirror", mates)
     work = lax.ppermute(targets, "mirror", swap_pairs())[0]
+    n = colloc.shape[0] // 2
+    core = lax.rem(lax.axis_index("mirror"), 2)
+    half = lax.dynamic_slice(colloc, (core * n, 0), (n, colloc.shape[1]))
     rows = pl.pallas_call(
         pick_kernel,
-        out_shape=shape((colloc.shape[0] // 2, 2 * nb), f32),
-        in_specs=[SMEM, SMEM, ANY],
+        out_shape=shape((n, 2 * nb), f32),
+        in_specs=[SMEM, SMEM, VMEM],
         out_specs=VMEM,
-        scratch_shapes=[pltpu.SemaphoreType.DMA((2,))],
         compiler_params=params(8),
         name="pick",
-    )(pair_list, mate, colloc)
-
-    z_groups = [[x * NZ + z for z in range(NZ)] for x in range(NX)]
-    own = lax.all_gather(rows, "blk", axis=0, tiled=True, axis_index_groups=z_groups)
-    h = own.shape[0] // 2
-    side0 = lax.ppermute(own[:h], "blk", x_trade(3))
-    near1 = lax.ppermute(own[h:], "blk", x_trade(1))
-    side1 = lax.ppermute(own[h:], "blk", x_trade(3))
-    near0 = lax.ppermute(own[:h], "blk", x_trade(1))
+    )(pair_list[:, ::-1], mate, half)
+
+    z1 = lax.ppermute(rows, "blk", z_trade(1))
+    z3 = lax.ppermute(rows, "blk", z_trade(3))
+    z2 = lax.ppermute(rows, "blk", z_trade(2))
+    early = jnp.concatenate([rows, z1], axis=0)
+    late = jnp.concatenate([z2, z3], axis=0)
+    side0 = lax.ppermute(early, "blk", x_trade(3))
+    near0 = lax.ppermute(early, "blk", x_trade(1))
+    near1 = lax.ppermute(late, "blk", x_trade(1))
+    side1 = lax.ppermute(late, "blk", x_trade(3))
+    far0 = lax.ppermute(side0, "blk", x_trade(1))
     far1 = lax.ppermute(near1, "blk", x_trade(3))
-    far0 = lax.ppermute(side0, "blk", x_trade(1))
 
     unit = 2 * 1024 * 2048 * 128
     weights = [pltpu.VMEM((naux * nb, 512), bf16)] * 2
     acc, lt0, rt0 = pl.pallas_call(
         fit_first_kernel,
         out_shape=(shape((naux * nb, 2 * nb), f32), shape((nb, 1536), f32), shape((2 * nb, 1536), bf16)),
-        in_specs=[VMEM] * 6,
+        in_specs=[VMEM] * 9,
         out_specs=[VMEM] * 3,
         scratch_shapes=weights,
         compiler_params=params(16),
         cost_estimate=cost(3 * unit, 5),
         name="fit_first",
-    )(own, near0, near1, side0, side1, coeffs)
+    )(rows, z1, z2, z3, near0, near1, side0, side1, coeffs)
     u, lt1, rt1 = pl.pallas_call(
         fit_last_kernel,
         out_shape=(shape((naux, nb, nb), f32), shape((nb, 512), f32), shape((2 * nb, 512), bf16)),
@@ -201,11 +201,11 @@
     )(far0, far1, acc, coeffs, work)
 
     other = lax.ppermute(u, "mirror", mates)
-    half = shape((NY, naux, nb), f32)
+    eight = shape((NY, naux, nb), f32)
     stacked = shape((naux * nb, 2 * nb), bf16)
     send, hh, ll, res = pl.pallas_call(
         send_kernel,
-        out_shape=(half, stacked, stacked, shape((naux, nb, nb), f32)),
+        out_shape=(eight, stacked, stacked, shape((naux, nb, nb), f32)),
         in_specs=[VMEM] * 6,
         out_specs=[VMEM] * 4,
         compiler_params=params(16),
@@ -216,7 +216,7 @@
     moved = lax.ppermute(send, "mirror", [(m, m ^ NC) for m in range(MIRROR)])
     keep = pl.pallas_call(
         keep_kernel,
-        out_shape=half,
+        out_shape=eight,
         in_specs=[VMEM] * 6,
         out_specs=VMEM,
         compiler_params=params(16),

time: 88.9 us -> 84.5 us (0.951)
  the two profiles are of different devices: /device:TPU:1 before, /device:TPU:64 now
where the time goes in v3:
time: 84.5 us; the launch traced here: 84 us
  starting transfers between devices  45 us (53%)
  blocking collectives  16.2 us (19%)
  waiting for transfers between devices  13.8 us (16%)
  Pallas kernels  5.86 us (7%)
  local copies, waits for them, and re-layouts  1.64 us (2%)
  between operations  0.86 us (1%)
    all_to_all x1, blocking collectives, per_device(): lax.all_to_all(keep + moved, 'mirror', 0, 0, tiled=True, axis_index_group...  16.2 us
    ppermute x1, starting transfers between devices, per_device(): moved = lax.ppermute(send, 'mirror', [(m, m ^ NC) for m in range(MIRROR)])  9.28 us
    ppermute x1, starting transfers between devices, per_device(): z2 = lax.ppermute(rows, 'blk', z_trade(2))  6.09 us
    ppermute x1, starting transfers between devices, per_device(): z3 = lax.ppermute(rows, 'blk', z_trade(3))  4.22 us
    ppermute x1, starting transfers between devices, per_device(): side0 = lax.ppermute(early, 'blk', x_trade(3))  3.83 us
    ppermute x1, starting transfers between devices, per_device(): far0 = lax.ppermute(side0, 'blk', x_trade(1))  3.32 us
    ppermute x1, starting transfers between devices, per_device(): side1 = lax.ppermute(late, 'blk', x_trade(3))  3.23 us
    ppermute x1, starting transfers between devices, per_device(): far1 = lax.ppermute(near1, 'blk', x_trade(3))  3.03 us
  transfers between devices with their start and end apart: 14, of which 9 were waited for; matrix products, arithmetic and copies ran while one was open for 2% of the time, Pallas kernels for 4%

profile of v3, /device:TPU:64, one launch (start us, length us, event | category | flops | bytes accessed | tf_op | source)
XLA Modules:
  0.0 84.0 jit_solution(8232538077851177850)
XLA Ops:
  0.7 2.1 %collective-permute-start = (s32[1,2]{1,0:T(1,128)}, s32[1,2]{1,0:T(1,128)S(1)}, u32[]{:S(2)}, u32[]{:S(2)}) collective-permute-start(s32[1,2]{1,0:T(1,128)} %param.7), channel_id=1, source_target_pairs={{0,16},{16,0},{32,48},{48,32},{64,80},{80,64},{96,112},{112,96},{1... | collective-permute-start | bytes 32 | tf_op jit(solution)/shard_map/ppermute | solution.py:154
  4.5 6.1 %collective-permute-start.4 = (f32[128,256]{1,0:T(8,128)S(1)}, f32[128,256]{1,0:T(8,128)S(1)}, u32[]{:S(2)}, u32[]{:S(2)}) collective-permute-start(f32[128,256]{1,0:T(8,128)S(1)} %pick.1.own0), channel_id=1, source_target_pairs={{0,2},{1,3},{2,0},{3,1},{4,6},{5,7},{6,4},{7,5},{8,10},{9,11},{10,... | collective-permute-start | bytes 393224 | tf_op jit(solution)/shard_map/ppermute | solution.py:170
  10.6 4.2 %collective-permute-start.5 = (f32[128,256]{1,0:T(8,128)S(1)}, f32[128,256]{1,0:T(8,128)S(1)}, u32[]{:S(2)}, u32[]{:S(2)}) collective-permute-start(f32[128,256]{1,0:T(8,128)S(1)} %pick.1.own0), channel_id=1, source_target_pairs={{0,3},{1,2},{2,1},{3,0},{4,7},{5,6},{6,5},{7,4},{8,11},{9,10},{10,... | collective-permute-start | bytes 393224 | tf_op jit(solution)/shard_map/ppermute | solution.py:169
  15.6 1.9 %collective-permute-start.1 = (f32[128,256]{1,0:T(8,128)S(1)}, f32[128,256]{1,0:T(8,128)S(1)}, u32[]{:S(2)}, u32[]{:S(2)}) collective-permute-start(f32[128,256]{1,0:T(8,128)S(1)} %pick.1.own0), channel_id=1, source_target_pairs={{0,1},{1,0},{2,3},{3,2},{4,5},{5,4},{6,7},{7,6},{8,9},{9,8},{10,11... | collective-permute-start | bytes 393224 | tf_op jit(solution)/shard_map/ppermute | solution.py:168
  17.5 2.5 %collective-permute-done.4.own2 = f32[128,256]{1,0:T(8,128)S(1)} collective-permute-done((f32[128,256]{1,0:T(8,128)S(1)}, f32[128,256]{1,0:T(8,128)S(1)}, u32[]{:S(2)}, u32[]{:S(2)}) %collective-permute-start.4) | collective-permute-done | bytes 131104 | tf_op jit(solution)/shard_map/ppermute | solution.py:170
  20.0 2.9 %collective-permute-done.5.own3 = f32[128,256]{1,0:T(8,128)S(1)} collective-permute-done((f32[128,256]{1,0:T(8,128)S(1)}, f32[128,256]{1,0:T(8,128)S(1)}, u32[]{:S(2)}, u32[]{:S(2)}) %collective-permute-start.5) | collective-permute-done | bytes 131104 | tf_op jit(solution)/shard_map/ppermute | solution.py:169
  22.9 1.9 %collective-permute-start.6 = (f32[256,256]{1,0:T(8,128)S(1)}, f32[256,256]{1,0:T(8,128)S(1)}, u32[]{:S(2)}, u32[]{:S(2)}) collective-permute-start(f32[256,256]{1,0:T(8,128)S(1)} %constant_dynamic-update-slice_fusion), channel_id=1, source_target_pairs={{0,4},{1,5},{2,6},{3,7},{4,0},{5,1},{6,2},{7,3},{8,12},{9,13},{10,... | collective-permute-start | bytes 786440 | tf_op jit(solution)/shard_map/ppermute | solution.py:175
  24.9 3.8 %collective-permute-start.2 = (f32[256,256]{1,0:T(8,128)S(1)}, f32[256,256]{1,0:T(8,128)S(1)}, u32[]{:S(2)}, u32[]{:S(2)}) collective-permute-start(f32[256,256]{1,0:T(8,128)S(1)} %pad_maximum_fusion), channel_id=1, source_target_pairs={{0,12},{1,13},{2,14},{3,15},{4,8},{5,9},{6,10},{7,11},{8,4},{9,5},... | collective-permute-start | bytes 786440 | tf_op jit(solution)/shard_map/ppermute | solution.py:173
  28.7 3.2 %collective-permute-start.9 = (f32[256,256]{1,0:T(8,128)S(1)}, f32[256,256]{1,0:T(8,128)S(1)}, u32[]{:S(2)}, u32[]{:S(2)}) collective-permute-start(f32[256,256]{1,0:T(8,128)S(1)} %constant_dynamic-update-slice_fusion), channel_id=1, source_target_pairs={{0,12},{1,13},{2,14},{3,15},{4,8},{5,9},{6,10},{7,11},{8,4},{9,5},... | collective-permute-start | bytes 786440 | tf_op jit(solution)/shard_map/ppermute | solution.py:176
  31.9 2.7 %collective-permute-start.8 = (f32[256,256]{1,0:T(8,128)S(1)}, f32[256,256]{1,0:T(8,128)S(1)}, u32[]{:S(2)}, u32[]{:S(2)}) collective-permute-start(f32[256,256]{1,0:T(8,128)S(1)} %pad_maximum_fusion), channel_id=1, source_target_pairs={{0,4},{1,5},{2,6},{3,7},{4,0},{5,1},{6,2},{7,3},{8,12},{9,13},{10,... | collective-permute-start | bytes 786440 | tf_op jit(solution)/shard_map/ppermute | solution.py:174
  34.7 3.0 %collective-permute-start.7 = (f32[256,256]{1,0:T(8,128)S(1)}, f32[256,256]{1,0:T(8,128)S(1)}, u32[]{:S(2)}, u32[]{:S(2)}) collective-permute-start(f32[256,256]{1,0:T(8,128)S(1)} %collective-permute-done.6.near1), channel_id=1, source_target_pairs={{0,12},{1,13},{2,14},{3,15},{4,8},{5,9},{6,10},{7,11},{8,4},{9,5},... | collective-permute-start | bytes 786440 | tf_op jit(solution)/shard_map/ppermute | solution.py:178
  37.7 3.3 %collective-permute-start.3 = (f32[256,256]{1,0:T(8,128)S(1)}, f32[256,256]{1,0:T(8,128)S(1)}, u32[]{:S(2)}, u32[]{:S(2)}) collective-permute-start(f32[256,256]{1,0:T(8,128)S(1)} %collective-permute-done.2.side0), channel_id=1, source_target_pairs={{0,4},{1,5},{2,6},{3,7},{4,0},{5,1},{6,2},{7,3},{8,12},{9,13},{10,... | collective-permute-start | bytes 786440 | tf_op jit(solution)/shard_map/ppermute | solution.py:177
  41.1 0.9 %collective-permute-done.9.side1 = f32[256,256]{1,0:T(8,128)S(1)} collective-permute-done((f32[256,256]{1,0:T(8,128)S(1)}, f32[256,256]{1,0:T(8,128)S(1)}, u32[]{:S(2)}, u32[]{:S(2)}) %collective-permute-start.9) | collective-permute-done | bytes 262176 | tf_op jit(solution)/shard_map/ppermute | solution.py:176
  41.9 0.8 collective-permute-done.8.near0
  42.7 1.9 %fit_first.1 = (f32[1024,256]{1,0:T(8,128)S(1)}, f32[128,1536]{1,0:T(8,128)S(1)}, bf16[256,1536]{1,0:T(8,128)(2,1)S(1)}) custom-call(f32[128,256]{1,0:T(8,128)S(1)} %pick.1.own0, f32[128,256]{1,0:T(8,128)S(1)} %collective-permute-done.1.own1, f32[128,256]{1,0:T(8,128)S(1)} %collective-permute-done.4.own2, f32[128,256]{1,0:T(8,128)S(1)} %collective-permute-done.5.own3, ...), custom_call_target="tpu_custom_call" | custom-call | flops 1610612736 | bytes 5242880 | tf_op jit(solution)/shard_map/fit_first/pallas_call | solution.py:182
  44.6 3.0 %collective-permute-done.7.far1 = f32[256,256]{1,0:T(8,128)S(1)} collective-permute-done((f32[256,256]{1,0:T(8,128)S(1)}, f32[256,256]{1,0:T(8,128)S(1)}, u32[]{:S(2)}, u32[]{:S(2)}) %collective-permute-start.7) | collective-permute-done | bytes 262176 | tf_op jit(solution)/shard_map/ppermute | solution.py:178
  47.5 1.0 %collective-permute-done.3.far0 = f32[256,256]{1,0:T(8,128)S(1)} collective-permute-done((f32[256,256]{1,0:T(8,128)S(1)}, f32[256,256]{1,0:T(8,128)S(1)}, u32[]{:S(2)}, u32[]{:S(2)}) %collective-permute-start.3) | collective-permute-done | bytes 262176 | tf_op jit(solution)/shard_map/ppermute | solution.py:177
  49.3 2.0 %collective-permute-start.11 = (f32[8,128,128]{2,1,0:T(8,128)S(1)}, f32[8,128,128]{2,1,0:T(8,128)S(1)}, u32[]{:S(2)}, u32[]{:S(2)}) collective-permute-start(f32[8,128,128]{2,1,0:T(8,128)S(1)} %get-tuple-element.13.u_ref), channel_id=1, source_target_pairs={{0,16},{16,0},{32,48},{48,32},{64,80},{80,64},{96,112},{112,96},{1... | collective-permute-start | bytes 1572872 | tf_op jit(solution)/shard_map/ppermute | solution.py:203
  51.3 1.8 %collective-permute-done.11.o_ref = f32[8,128,128]{2,1,0:T(8,128)S(1)} collective-permute-done((f32[8,128,128]{2,1,0:T(8,128)S(1)}, f32[8,128,128]{2,1,0:T(8,128)S(1)}, u32[]{:S(2)}, u32[]{:S(2)}) %collective-permute-start.11) | collective-permute-done | bytes 524320 | tf_op jit(solution)/shard_map/ppermute | solution.py:203
  53.1 1.4 %gradient_send.1 = (f32[8,8,128]{2,1,0:T(8,128)S(1)}, bf16[1024,256]{1,0:T(8,128)(2,1)S(1)}, bf16[1024,256]{1,0:T(8,128)(2,1)S(1)}, f32[8,128,128]{2,1,0:T(8,128)S(1)}) custom-call(f32[8,128,128]{2,1,0:T(8,128)S(1)} %get-tuple-element.13.u_ref, f32[8,128,128]{2,1,0:T(8,128)S(1)} %collective-permute-done.11.o_ref, f32[128,1536]{1,0:T(8,128)S(1)} %get-tuple-element.14.lt0, ...), custom_call_target="tpu_custom_call" | custom-call | flops 1073741824 | bytes 4194304 | tf_op jit(solution)/shard_map/gradient_send/pallas_call | solution.py:206
  55.1 9.3 %collective-permute-start.13 = (f32[8,8,128]{2,1,0:T(8,128)S(1)}, f32[8,8,128]{2,1,0:T(8,128)S(1)}, u32[]{:S(2)}, u32[]{:S(2)}) collective-permute-start(f32[8,8,128]{2,1,0:T(8,128)S(1)} %get-tuple-element.21), channel_id=1, source_target_pairs={{0,32},{16,48},{32,0},{48,16},{64,96},{80,112},{96,64},{112,80},{1... | collective-permute-start | bytes 98312 | tf_op jit(solution)/shard_map/ppermute | solution.py:216
  64.4 1.3 %gradient_keep.1 = f32[8,8,128]{2,1,0:T(8,128)S(1)} custom-call(f32[128,1536]{1,0:T(8,128)S(1)} %get-tuple-element.14.lt0, f32[128,512]{1,0:T(8,128)S(1)} %get-tuple-element.15.lt1, bf16[256,1536]{1,0:T(8,128)(2,1)S(1)} %get-tuple-element.16.rt0, bf16[256,512]{1,0:T(8,128)(2,1)S(1)} %get-tuple-element.17.rt1, ...), custom_call_target="tpu_custom_call" | custom-call | flops 1073741824 | bytes 4194304 | tf_op jit(solution)/shard_map/gradient_keep/pallas_call | solution.py:217
  66.4 16.2 %all_to_all.5 = f32[8,8,128]{2,1,0:T(8,128)S(1)} all-to-all(f32[8,8,128]{2,1,0:T(8,128)S(1)} %add.7), channel_id=1, replica_groups={{0,64,128,192,256,320,384,448},{16,80,144,208,272,336,400,464},{32,96,1..., dimensions={0} | all-to-all | bytes 65536 | tf_op jit(solution)/shard_map/all_to_all | solution.py:227
  83.2 0.8 copy.8
  (24 shorter events, 5.3 us)
Async XLA Ops:
  0.6 2.8 %copy-start = (f32[256,2048]{1,0:T(8,128)S(1)}, f32[256,2048]{1,0:T(8,128)}, u32[]{:S(2)}) copy-start(f32[256,2048]{1,0:T(8,128)} %param.4) | copy-start | bytes 6291460
  0.6 14.2 %copy-start.2 = (f32[1,8,128,128]{3,2,1,0:T(8,128)S(1)}, f32[1,8,128,128]{3,2,1,0:T(8,128)}, u32[]{:S(2)}) copy-start(f32[1,8,128,128]{3,2,1,0:T(8,128)} %param.6) | copy-start | bytes 1572868
  0.7 3.3 %collective-permute-start = (s32[1,2]{1,0:T(1,128)}, s32[1,2]{1,0:T(1,128)S(1)}, u32[]{:S(2)}, u32[]{:S(2)}) collective-permute-start(s32[1,2]{1,0:T(1,128)} %param.7), channel_id=1, source_target_pairs={{0,16},{16,0},{32,48},{48,32},{64,80},{80,64},{96,112},{112,96},{1... | collective-permute-start | bytes 32 | tf_op jit(solution)/shard_map/ppermute | solution.py:154
  3.5 39.2 %copy-start.1 = (f32[8,4096]{1,0:T(8,128)S(1)}, f32[8,4096]{1,0:T(8,128)}, u32[]{:S(2)}) copy-start(f32[8,4096]{1,0:T(8,128)} %coef_ref.3) | copy-start | bytes 393220
  4.5 15.5 %collective-permute-start.4 = (f32[128,256]{1,0:T(8,128)S(1)}, f32[128,256]{1,0:T(8,128)S(1)}, u32[]{:S(2)}, u32[]{:S(2)}) collective-permute-start(f32[128,256]{1,0:T(8,128)S(1)} %pick.1.own0), channel_id=1, source_target_pairs={{0,2},{1,3},{2,0},{3,1},{4,6},{5,7},{6,4},{7,5},{8,10},{9,11},{10,... | collective-permute-start | bytes 393224 | tf_op jit(solution)/shard_map/ppermute | solution.py:170
  10.6 12.3 %collective-permute-start.5 = (f32[128,256]{1,0:T(8,128)S(1)}, f32[128,256]{1,0:T(8,128)S(1)}, u32[]{:S(2)}, u32[]{:S(2)}) collective-permute-start(f32[128,256]{1,0:T(8,128)S(1)} %pick.1.own0), channel_id=1, source_target_pairs={{0,3},{1,2},{2,1},{3,0},{4,7},{5,6},{6,5},{7,4},{8,11},{9,10},{10,... | collective-permute-start | bytes 393224 | tf_op jit(solution)/shard_map/ppermute | solution.py:169
  14.9 29.7 %collective-permute-start.10 = (f32[1,8,128,128]{3,2,1,0:T(8,128)S(1)}, f32[1,8,128,128]{3,2,1,0:T(8,128)S(1)}, u32[]{:S(2)}, u32[]{:S(2)}) collective-permute-start(f32[1,8,128,128]{3,2,1,0:T(8,128)S(1)} %copy-done.2), channel_id=1, source_target_pairs={{0,0},{16,256},{32,32},{48,288},{64,64},{80,320},{96,96},{112,352}... | collective-permute-start | bytes 1572872 | tf_op jit(solution)/shard_map/ppermute | solution.py:155
  15.6 9.3 %collective-permute-start.1 = (f32[128,256]{1,0:T(8,128)S(1)}, f32[128,256]{1,0:T(8,128)S(1)}, u32[]{:S(2)}, u32[]{:S(2)}) collective-permute-start(f32[128,256]{1,0:T(8,128)S(1)} %pick.1.own0), channel_id=1, source_target_pairs={{0,1},{1,0},{2,3},{3,2},{4,5},{5,4},{6,7},{7,6},{8,9},{9,8},{10,11... | collective-permute-start | bytes 393224 | tf_op jit(solution)/shard_map/ppermute | solution.py:168
  22.9 11.8 %collective-permute-start.6 = (f32[256,256]{1,0:T(8,128)S(1)}, f32[256,256]{1,0:T(8,128)S(1)}, u32[]{:S(2)}, u32[]{:S(2)}) collective-permute-start(f32[256,256]{1,0:T(8,128)S(1)} %constant_dynamic-update-slice_fusion), channel_id=1, source_target_pairs={{0,4},{1,5},{2,6},{3,7},{4,0},{5,1},{6,2},{7,3},{8,12},{9,13},{10,... | collective-permute-start | bytes 786440 | tf_op jit(solution)/shard_map/ppermute | solution.py:175
  24.9 12.8 %collective-permute-start.2 = (f32[256,256]{1,0:T(8,128)S(1)}, f32[256,256]{1,0:T(8,128)S(1)}, u32[]{:S(2)}, u32[]{:S(2)}) collective-permute-start(f32[256,256]{1,0:T(8,128)S(1)} %pad_maximum_fusion), channel_id=1, source_target_pairs={{0,12},{1,13},{2,14},{3,15},{4,8},{5,9},{6,10},{7,11},{8,4},{9,5},... | collective-permute-start | bytes 786440 | tf_op jit(solution)/shard_map/ppermute | solution.py:173
  28.7 13.2 %collective-permute-start.9 = (f32[256,256]{1,0:T(8,128)S(1)}, f32[256,256]{1,0:T(8,128)S(1)}, u32[]{:S(2)}, u32[]{:S(2)}) collective-permute-start(f32[256,256]{1,0:T(8,128)S(1)} %constant_dynamic-update-slice_fusion), channel_id=1, source_target_pairs={{0,12},{1,13},{2,14},{3,15},{4,8},{5,9},{6,10},{7,11},{8,4},{9,5},... | collective-permute-start | bytes 786440 | tf_op jit(solution)/shard_map/ppermute | solution.py:176
  31.9 10.7 %collective-permute-start.8 = (f32[256,256]{1,0:T(8,128)S(1)}, f32[256,256]{1,0:T(8,128)S(1)}, u32[]{:S(2)}, u32[]{:S(2)}) collective-permute-start(f32[256,256]{1,0:T(8,128)S(1)} %pad_maximum_fusion), channel_id=1, source_target_pairs={{0,4},{1,5},{2,6},{3,7},{4,0},{5,1},{6,2},{7,3},{8,12},{9,13},{10,... | collective-permute-start | bytes 786440 | tf_op jit(solution)/shard_map/ppermute | solution.py:174
  34.7 12.8 %collective-permute-start.7 = (f32[256,256]{1,0:T(8,128)S(1)}, f32[256,256]{1,0:T(8,128)S(1)}, u32[]{:S(2)}, u32[]{:S(2)}) collective-permute-start(f32[256,256]{1,0:T(8,128)S(1)} %collective-permute-done.6.near1), channel_id=1, source_target_pairs={{0,12},{1,13},{2,14},{3,15},{4,8},{5,9},{6,10},{7,11},{8,4},{9,5},... | collective-permute-start | bytes 786440 | tf_op jit(solution)/shard_map/ppermute | solution.py:178
  37.7 10.8 %collective-permute-start.3 = (f32[256,256]{1,0:T(8,128)S(1)}, f32[256,256]{1,0:T(8,128)S(1)}, u32[]{:S(2)}, u32[]{:S(2)}) collective-permute-start(f32[256,256]{1,0:T(8,128)S(1)} %collective-permute-done.2.side0), channel_id=1, source_target_pairs={{0,4},{1,5},{2,6},{3,7},{4,0},{5,1},{6,2},{7,3},{8,12},{9,13},{10,... | collective-permute-start | bytes 786440 | tf_op jit(solution)/shard_map/ppermute | solution.py:177
  49.3 3.8 %collective-permute-start.11 = (f32[8,128,128]{2,1,0:T(8,128)S(1)}, f32[8,128,128]{2,1,0:T(8,128)S(1)}, u32[]{:S(2)}, u32[]{:S(2)}) collective-permute-start(f32[8,128,128]{2,1,0:T(8,128)S(1)} %get-tuple-element.13.u_ref), channel_id=1, source_target_pairs={{0,16},{16,0},{32,48},{48,32},{64,80},{80,64},{96,112},{112,96},{1... | collective-permute-start | bytes 1572872 | tf_op jit(solution)/shard_map/ppermute | solution.py:203
  54.4 28.8 %collective-permute-start.12 = (f32[1,8,128,128]{3,2,1,0:T(8,128)S(1)}, f32[1,8,128,128]{3,2,1,0:T(8,128)S(1)}, u32[]{:S(2)}, u32[]{:S(2)}) collective-permute-start(f32[1,8,128,128]{3,2,1,0:T(8,128)S(1)} %bitcast.3), channel_id=1, source_target_pairs={{0,0},{16,256},{32,32},{48,288},{64,64},{80,320},{96,96},{112,352}... | collective-permute-start | bytes 1572872 | tf_op jit(solution)/shard_map/ppermute | solution.py:215
  55.1 11.3 %collective-permute-start.13 = (f32[8,8,128]{2,1,0:T(8,128)S(1)}, f32[8,8,128]{2,1,0:T(8,128)S(1)}, u32[]{:S(2)}, u32[]{:S(2)}) collective-permute-start(f32[8,8,128]{2,1,0:T(8,128)S(1)} %get-tuple-element.21), channel_id=1, source_target_pairs={{0,32},{16,48},{32,0},{48,16},{64,96},{80,112},{96,64},{112,80},{1... | collective-permute-start | bytes 98312 | tf_op jit(solution)/shard_map/ppermute | solution.py:216

commit v4 on v3

--- a/solution.py
+++ b/solution.py
@@ -66,11 +66,12 @@
         out_ref[:, k * 128 : (k + 1) * 128] = half_ref[:, pl.ds(pl.multiple_of(block * 128, 128), 128)]
 
 
-def fit_part(coef_ref, rows, xs, lt_ref, rt_ref, n, whi, wlo):
+def fit_part(coef_ref, rows, xs, zs, lt_ref, rt_ref, at, whi, wlo):
     core = lax.rem(lax.axis_index("mirror"), 2)
     left, right = rows[:, :128], rows[:, 128:]
     lt, rt = left.T, right.T
-    cols = pl.ds(n * 512, 512)
+    wide = rows.shape[0]
+    cols = pl.ds(at, wide)
     lt_ref[:, cols] = lt
     rhi, rlo = split(right)
     rthi, rtlo = split(rt)
@@ -78,33 +79,40 @@
     rt_ref[128:256, cols] = rtlo
     both = jnp.concatenate([rhi, rlo], axis=1)
     cs = []
-    for z in z_order(lax.rem(lax.axis_index("blk"), NZ)):
-        at = pl.multiple_of((xs * NZ + z) * 256 + core * 128, 128)
-        cs.append(coef_ref[:, pl.ds(at, 128)])
+    for z in zs:
+        start = pl.multiple_of((xs * NZ + z) * 256 + core * 128, 128)
+        cs.append(coef_ref[:, pl.ds(start, 128)])
     cf = jnp.concatenate(cs, axis=1)
     for a in range(coef_ref.shape[0]):
         hi, lo = split(cf[a : a + 1, :] * lt)
-        whi[pl.ds(a * 128, 128), :] = hi
-        wlo[pl.ds(a * 128, 128), :] = lo
-    part = jnp.dot(whi[...], both, preferred_element_type=f32)
-    return part + jnp.dot(wlo[...], both, preferred_element_type=f32)
+        whi[pl.ds(a * 128, 128), 0:wide] = hi
+        wlo[pl.ds(a * 128, 128), 0:wide] = lo
+    part = jnp.dot(whi[:, 0:wide], both, preferred_element_type=f32)
+    return part + jnp.dot(wlo[:, 0:wide], both, preferred_element_type=f32)
 
 
 def fit_first_kernel(own0, own1, own2, own3, near0, near1, side0, side1, coef_ref, acc_ref, lt_ref, rt_ref, whi, wlo):
     xs = sources(lax.axis_index("blk") // NZ)
+    zs = z_order(lax.rem(lax.axis_index("blk"), NZ))
     for n, refs in enumerate(((own0, own1, own2, own3), (near0, near1), (side0, side1))):
         rows = jnp.concatenate([r[...] for r in refs], axis=0)
-        part = fit_part(coef_ref, rows, xs[n], lt_ref, rt_ref, n, whi, wlo)
+        part = fit_part(coef_ref, rows, xs[n], zs, lt_ref, rt_ref, n * 512, whi, wlo)
         if n == 0:
             acc_ref[...] = part
         else:
             acc_ref[...] += part
 
 
-def fit_last_kernel(far0, far1, acc_ref, coef_ref, t_ref, u_ref, lt_ref, rt_ref, whi, wlo):
+def fit_next_kernel(far0, acc_ref, coef_ref, out_ref, lt_ref, rt_ref, whi, wlo):
     xs = sources(lax.axis_index("blk") // NZ)
-    rows = jnp.concatenate([far0[...], far1[...]], axis=0)
-    tot = acc_ref[...] + fit_part(coef_ref, rows, xs[3], lt_ref, rt_ref, 0, whi, wlo)
+    zs = z_order(lax.rem(lax.axis_index("blk"), NZ))
+    out_ref[...] = acc_ref[...] + fit_part(coef_ref, far0[...], xs[3], zs[:2], lt_ref, rt_ref, 0, whi, wlo)
+
+
+def fit_last_kernel(far1, acc_ref, coef_ref, t_ref, u_ref, lt_ref, rt_ref, whi, wlo):
+    xs = sources(lax.axis_index("blk") // NZ)
+    zs = z_order(lax.rem(lax.axis_index("blk"), NZ))
+    tot = acc_ref[...] + fit_part(coef_ref, far1[...], xs[3], zs[2:], lt_ref, rt_ref, 0, whi, wlo)
     fit = tot[:, :128] + tot[:, 128:]
     u_ref[...] = 0.5 * t_ref[...] - fit.reshape(t_ref.shape)
 
@@ -113,11 +121,10 @@
     z = lax.rem(lax.axis_index("blk"), NZ)
     first, pair = lax.rem(z + parity, 2), z // 2
     for n, xs in enumerate(sources(lax.axis_index("blk") // NZ)):
-        lt_ref, rt_ref = (lt_refs[0], rt_refs[0]) if n < 3 else (lt_refs[1], rt_refs[1])
-        at = n * 512 if n < 3 else 0
-        cols = [pl.ds(pl.multiple_of(at + j * 256 + first * 128, 128), 128) for j in range(2)]
-        rt = jnp.concatenate([rt_ref[:, c] for c in cols], axis=1)
-        lt = jnp.concatenate([lt_ref[:, c] for c in cols], axis=1)
+        places = [(0, n * 512 + j * 256) for j in range(2)] if n < 3 else [(1, 0), (2, 0)]
+        cols = [(i, pl.ds(pl.multiple_of(at + first * 128, 128), 128)) for i, at in places]
+        rt = jnp.concatenate([rt_refs[i][:, c] for i, c in cols], axis=1)
+        lt = jnp.concatenate([lt_refs[i][:, c] for i, c in cols], axis=1)
         spread = jnp.dot(hh[...], rt, preferred_element_type=f32)
         spread += jnp.dot(ll[...], rt, preferred_element_type=f32)
         terms = []
@@ -128,7 +135,7 @@
             out_ref[xs * 2 + (pair if j == 0 else 1 - pair)] = block[:, j * 128 : (j + 1) * 128]
 
 
-def send_kernel(u_ref, o_ref, lt0, lt1, rt0, rt1, out_ref, hh_ref, ll_ref, r_ref):
+def send_kernel(u_ref, o_ref, lt0, lt1, lt2, rt0, rt1, rt2, out_ref, hh_ref, ll_ref, r_ref):
     zh = lax.rem(lax.axis_index("mirror") // NC, NZH)
     for a in range(u_ref.shape[0]):
         r = u_ref[a] + o_ref[a].T
@@ -139,12 +146,12 @@
         hh_ref[rows, 128:256] = hi
         ll_ref[rows, 0:128] = lo
         ll_ref[rows, 128:256] = lo
-    blocks(1 - zh, (lt0, lt1), (rt0, rt1), out_ref, hh_ref, ll_ref)
-
-
-def keep_kernel(lt0, lt1, rt0, rt1, hh_ref, ll_ref, out_ref):
+    blocks(1 - zh, (lt0, lt1, lt2), (rt0, rt1, rt2), out_ref, hh_ref, ll_ref)
+
+
+def keep_kernel(lt0, lt1, lt2, rt0, rt1, rt2, hh_ref, ll_ref, out_ref):
     zh = lax.rem(lax.axis_index("mirror") // NC, NZH)
-    blocks(zh, (lt0, lt1), (rt0, rt1), out_ref, hh_ref, ll_ref)
+    blocks(zh, (lt0, lt1, lt2), (rt0, rt1, rt2), out_ref, hh_ref, ll_ref)
 
 
 def per_device(colloc, coeffs, targets, pair_list):
@@ -189,16 +196,26 @@
         cost_estimate=cost(3 * unit, 5),
         name="fit_first",
     )(rows, z1, z2, z3, near0, near1, side0, side1, coeffs)
-    u, lt1, rt1 = pl.pallas_call(
-        fit_last_kernel,
-        out_shape=(shape((naux, nb, nb), f32), shape((nb, 512), f32), shape((2 * nb, 512), bf16)),
-        in_specs=[VMEM] * 5,
+    acc, lt1, rt1 = pl.pallas_call(
+        fit_next_kernel,
+        out_shape=(shape((naux * nb, 2 * nb), f32), shape((nb, 256), f32), shape((2 * nb, 256), bf16)),
+        in_specs=[VMEM] * 3,
         out_specs=[VMEM] * 3,
         scratch_shapes=weights,
         compiler_params=params(16),
-        cost_estimate=cost(unit, 3),
+        cost_estimate=cost(unit // 2, 3),
+        name="fit_next",
+    )(far0, acc, coeffs)
+    u, lt2, rt2 = pl.pallas_call(
+        fit_last_kernel,
+        out_shape=(shape((naux, nb, nb), f32), shape((nb, 256), f32), shape((2 * nb, 256), bf16)),
+        in_specs=[VMEM] * 4,
+        out_specs=[VMEM] * 3,
+        scratch_shapes=weights,
+        compiler_params=params(16),
+        cost_estimate=cost(unit // 2, 3),
         name="fit_last",
-    )(far0, far1, acc, coeffs, work)
+    )(far1, acc, coeffs, work)
 
     other = lax.ppermute(u, "mirror", mates)
     eight = shape((NY, naux, nb), f32)
@@ -206,23 +223,23 @@
     send, hh, ll, res = pl.pallas_call(
         send_kernel,
         out_shape=(eight, stacked, stacked, shape((naux, nb, nb), f32)),
-        in_specs=[VMEM] * 6,
+        in_specs=[VMEM] * 8,
         out_specs=[VMEM] * 4,
         compiler_params=params(16),
         cost_estimate=cost(2 * unit, 4),
         name="gradient_send",
-    )(u, other, lt0, lt1, rt0, rt1)
+    )(u, other, lt0, lt1, lt2, rt0, rt1, rt2)
     residual = lax.ppermute(res[None], "mirror", swap_pairs())
     moved = lax.ppermute(send, "mirror", [(m, m ^ NC) for m in range(MIRROR)])
     keep = pl.pallas_call(
         keep_kernel,
         out_shape=eight,
-        in_specs=[VMEM] * 6,
+        in_specs=[VMEM] * 8,
         out_specs=VMEM,
         compiler_params=params(16),
         cost_estimate=cost(2 * unit, 4),
         name="gradient_keep",
-    )(lt0, lt1, rt0, rt1, hh, ll)
+    )(lt0, lt1, lt2, rt0, rt1, rt2, hh, ll)
     y_groups = [[(y * NZH + h) * NC + c for y in range(NY)] for h in range(NZH) for c in range(NC)]
     spread = lax.all_to_all(keep + moved, "mirror", 0, 0, tiled=True, axis_index_groups=y_groups)
     return residual, jnp.sum(spread, axis=0)

time: 84.5 us -> 84 us (level)
  the two profiles are of different devices: /device:TPU:64 before, /device:TPU:1 now
where the time goes in v4:
time: 84 us; the launch traced here: 83.5 us
  starting transfers between devices  57.4 us (68%)
  blocking collectives  10.5 us (12%)
  waiting for transfers between devices  6.35 us (8%)
  Pallas kernels  6.08 us (7%)
  local copies, waits for them, and re-layouts  1.64 us (2%)
  between operations  0.91 us (1%)
    all_to_all x1, blocking collectives, per_device(): lax.all_to_all(keep + moved, 'mirror', 0, 0, tiled=True, axis_index_group...  10.5 us
    ppermute x1, starting transfers between devices, per_device(): mate = lax.ppermute(pair_list, 'mirror', mates)  8.92 us
    ppermute x1, starting transfers between devices, per_device(): work = lax.ppermute(targets, 'mirror', swap_pairs())[0]  8.2 us
    ppermute x1, starting transfers between devices, per_device(): moved = lax.ppermute(send, 'mirror', [(m, m ^ NC) for m in range(MIRROR)])  7.93 us
    ppermute x1, starting transfers between devices, per_device(): residual = lax.ppermute(res[None], 'mirror', swap_pairs())  5.39 us
    ppermute x1, starting transfers between devices, per_device(): side0 = lax.ppermute(early, 'blk', x_trade(3))  4.39 us
    ppermute x1, starting transfers between devices, per_device(): side1 = lax.ppermute(late, 'blk', x_trade(3))  4.39 us
    ppermute x1, starting transfers between devices, per_device(): near1 = lax.ppermute(late, 'blk', x_trade(1))  3.12 us
  transfers between devices with their start and end apart: 14, of which 5 were waited for; matrix products, arithmetic and copies ran while one was open for 2% of the time, Pallas kernels for 4%

profile of v4, /device:TPU:1, one launch (start us, length us, event | category | flops | bytes accessed | tf_op | source)
XLA Modules:
  0.0 83.5 jit_solution(2279366466129211626)
XLA Ops:
  0.7 8.9 %collective-permute-start = (s32[1,2]{1,0:T(1,128)}, s32[1,2]{1,0:T(1,128)S(1)}, u32[]{:S(2)}, u32[]{:S(2)}) collective-permute-start(s32[1,2]{1,0:T(1,128)} %param.7), channel_id=1, source_target_pairs={{0,16},{16,0},{32,48},{48,32},{64,80},{80,64},{96,112},{112,96},{1... | collective-permute-start | bytes 32 | tf_op jit(solution)/shard_map/ppermute | solution.py:161
  9.6 0.7 rev.3.mine_ref
  11.1 1.9 %collective-permute-start.5 = (f32[128,256]{1,0:T(8,128)S(1)}, f32[128,256]{1,0:T(8,128)S(1)}, u32[]{:S(2)}, u32[]{:S(2)}) collective-permute-start(f32[128,256]{1,0:T(8,128)S(1)} %pick.1.own0), channel_id=1, source_target_pairs={{0,1},{1,0},{2,3},{3,2},{4,5},{5,4},{6,7},{7,6},{8,9},{9,8},{10,11... | collective-permute-start | bytes 393224 | tf_op jit(solution)/shard_map/ppermute | solution.py:175
  13.0 2.5 %collective-permute-start.1 = (f32[128,256]{1,0:T(8,128)S(1)}, f32[128,256]{1,0:T(8,128)S(1)}, u32[]{:S(2)}, u32[]{:S(2)}) collective-permute-start(f32[128,256]{1,0:T(8,128)S(1)} %pick.1.own0), channel_id=1, source_target_pairs={{0,2},{1,3},{2,0},{3,1},{4,6},{5,7},{6,4},{7,5},{8,10},{9,11},{10,... | collective-permute-start | bytes 393224 | tf_op jit(solution)/shard_map/ppermute | solution.py:177
  15.6 8.2 %collective-permute-start.10 = (f32[1,8,128,128]{3,2,1,0:T(8,128)S(1)}, f32[1,8,128,128]{3,2,1,0:T(8,128)S(1)}, u32[]{:S(2)}, u32[]{:S(2)}) collective-permute-start(f32[1,8,128,128]{3,2,1,0:T(8,128)S(1)} %copy-done.2), channel_id=1, source_target_pairs={{0,0},{16,256},{32,32},{48,288},{64,64},{80,320},{96,96},{112,352}... | collective-permute-start | bytes 1572872 | tf_op jit(solution)/shard_map/ppermute | solution.py:162
  23.8 1.9 %collective-permute-start.2 = (f32[128,256]{1,0:T(8,128)S(1)}, f32[128,256]{1,0:T(8,128)S(1)}, u32[]{:S(2)}, u32[]{:S(2)}) collective-permute-start(f32[128,256]{1,0:T(8,128)S(1)} %pick.1.own0), channel_id=1, source_target_pairs={{0,3},{1,2},{2,1},{3,0},{4,7},{5,6},{6,5},{7,4},{8,11},{9,10},{10,... | collective-permute-start | bytes 393224 | tf_op jit(solution)/shard_map/ppermute | solution.py:176
  25.7 4.4 %collective-permute-start.6 = (f32[256,256]{1,0:T(8,128)S(1)}, f32[256,256]{1,0:T(8,128)S(1)}, u32[]{:S(2)}, u32[]{:S(2)}) collective-permute-start(f32[256,256]{1,0:T(8,128)S(1)} %pad_maximum_fusion), channel_id=1, source_target_pairs={{0,12},{1,13},{2,14},{3,15},{4,8},{5,9},{6,10},{7,11},{8,4},{9,5},... | collective-permute-start | bytes 786440 | tf_op jit(solution)/shard_map/ppermute | solution.py:180
  30.2 1.1 %collective-permute-done.2.own3 = f32[128,256]{1,0:T(8,128)S(1)} collective-permute-done((f32[128,256]{1,0:T(8,128)S(1)}, f32[128,256]{1,0:T(8,128)S(1)}, u32[]{:S(2)}, u32[]{:S(2)}) %collective-permute-start.2) | collective-permute-done | bytes 131104 | tf_op jit(solution)/shard_map/ppermute | solution.py:176
  31.3 3.1 %collective-permute-start.3 = (f32[256,256]{1,0:T(8,128)S(1)}, f32[256,256]{1,0:T(8,128)S(1)}, u32[]{:S(2)}, u32[]{:S(2)}) collective-permute-start(f32[256,256]{1,0:T(8,128)S(1)} %constant_dynamic-update-slice_fusion), channel_id=1, source_target_pairs={{0,4},{1,5},{2,6},{3,7},{4,0},{5,1},{6,2},{7,3},{8,12},{9,13},{10,... | collective-permute-start | bytes 786440 | tf_op jit(solution)/shard_map/ppermute | solution.py:182
  34.4 2.2 %collective-permute-start.8 = (f32[256,256]{1,0:T(8,128)S(1)}, f32[256,256]{1,0:T(8,128)S(1)}, u32[]{:S(2)}, u32[]{:S(2)}) collective-permute-start(f32[256,256]{1,0:T(8,128)S(1)} %pad_maximum_fusion), channel_id=1, source_target_pairs={{0,4},{1,5},{2,6},{3,7},{4,0},{5,1},{6,2},{7,3},{8,12},{9,13},{10,... | collective-permute-start | bytes 786440 | tf_op jit(solution)/shard_map/ppermute | solution.py:181
  36.6 4.4 %collective-permute-start.9 = (f32[256,256]{1,0:T(8,128)S(1)}, f32[256,256]{1,0:T(8,128)S(1)}, u32[]{:S(2)}, u32[]{:S(2)}) collective-permute-start(f32[256,256]{1,0:T(8,128)S(1)} %constant_dynamic-update-slice_fusion), channel_id=1, source_target_pairs={{0,12},{1,13},{2,14},{3,15},{4,8},{5,9},{6,10},{7,11},{8,4},{9,5},... | collective-permute-start | bytes 786440 | tf_op jit(solution)/shard_map/ppermute | solution.py:183
  41.0 1.9 %collective-permute-start.7 = (f32[256,256]{1,0:T(8,128)S(1)}, f32[256,256]{1,0:T(8,128)S(1)}, u32[]{:S(2)}, u32[]{:S(2)}) collective-permute-start(f32[256,256]{1,0:T(8,128)S(1)} %collective-permute-done.6.side0), channel_id=1, source_target_pairs={{0,4},{1,5},{2,6},{3,7},{4,0},{5,1},{6,2},{7,3},{8,12},{9,13},{10,... | collective-permute-start | bytes 786440 | tf_op jit(solution)/shard_map/ppermute | solution.py:184
  42.9 2.7 %collective-permute-start.4 = (f32[256,256]{1,0:T(8,128)S(1)}, f32[256,256]{1,0:T(8,128)S(1)}, u32[]{:S(2)}, u32[]{:S(2)}) collective-permute-start(f32[256,256]{1,0:T(8,128)S(1)} %collective-permute-done.3.near1), channel_id=1, source_target_pairs={{0,12},{1,13},{2,14},{3,15},{4,8},{5,9},{6,10},{7,11},{8,4},{9,5},... | collective-permute-start | bytes 786440 | tf_op jit(solution)/shard_map/ppermute | solution.py:185
  45.7 0.7 collective-permute-done.9.side1
  46.4 1.9 %fit_first.1 = (f32[1024,256]{1,0:T(8,128)S(1)}, f32[128,1536]{1,0:T(8,128)S(1)}, bf16[256,1536]{1,0:T(8,128)(2,1)S(1)}) custom-call(f32[128,256]{1,0:T(8,128)S(1)} %pick.1.own0, f32[128,256]{1,0:T(8,128)S(1)} %collective-permute-done.5.own1, f32[128,256]{1,0:T(8,128)S(1)} %collective-permute-done.1.own2, f32[128,256]{1,0:T(8,128)S(1)} %collective-permute-done.2.own3, ...), custom_call_target="tpu_custom_call" | custom-call | flops 1610612736 | bytes 5242880 | tf_op jit(solution)/shard_map/fit_first/pallas_call | solution.py:189
  48.8 2.5 %collective-permute-done.4.far1 = f32[256,256]{1,0:T(8,128)S(1)} collective-permute-done((f32[256,256]{1,0:T(8,128)S(1)}, f32[256,256]{1,0:T(8,128)S(1)}, u32[]{:S(2)}, u32[]{:S(2)}) %collective-permute-start.4) | collective-permute-done | bytes 262176 | tf_op jit(solution)/shard_map/ppermute | solution.py:185
  51.8 1.9 %collective-permute-start.11 = (f32[8,128,128]{2,1,0:T(8,128)S(1)}, f32[8,128,128]{2,1,0:T(8,128)S(1)}, u32[]{:S(2)}, u32[]{:S(2)}) collective-permute-start(f32[8,128,128]{2,1,0:T(8,128)S(1)} %get-tuple-element.17.u_ref), channel_id=1, source_target_pairs={{0,16},{16,0},{32,48},{48,32},{64,80},{80,64},{96,112},{112,96},{1... | collective-permute-start | bytes 1572872 | tf_op jit(solution)/shard_map/ppermute | solution.py:220
  53.7 1.9 %collective-permute-done.11.o_ref = f32[8,128,128]{2,1,0:T(8,128)S(1)} collective-permute-done((f32[8,128,128]{2,1,0:T(8,128)S(1)}, f32[8,128,128]{2,1,0:T(8,128)S(1)}, u32[]{:S(2)}, u32[]{:S(2)}) %collective-permute-start.11) | collective-permute-done | bytes 524320 | tf_op jit(solution)/shard_map/ppermute | solution.py:220
  55.6 1.4 %gradient_send.1 = (f32[8,8,128]{2,1,0:T(8,128)S(1)}, bf16[1024,256]{1,0:T(8,128)(2,1)S(1)}, bf16[1024,256]{1,0:T(8,128)(2,1)S(1)}, f32[8,128,128]{2,1,0:T(8,128)S(1)}) custom-call(f32[8,128,128]{2,1,0:T(8,128)S(1)} %get-tuple-element.17.u_ref, f32[8,128,128]{2,1,0:T(8,128)S(1)} %collective-permute-done.11.o_ref, f32[128,1536]{1,0:T(8,128)S(1)} %get-tuple-element.18.lt0, ...), custom_call_target="tpu_custom_call" | custom-call | flops 1073741824 | bytes 4194304 | tf_op jit(solution)/shard_map/gradient_send/pallas_call | solution.py:223
  56.9 5.4 %collective-permute-start.12 = (f32[1,8,128,128]{3,2,1,0:T(8,128)S(1)}, f32[1,8,128,128]{3,2,1,0:T(8,128)S(1)}, u32[]{:S(2)}, u32[]{:S(2)}) collective-permute-start(f32[1,8,128,128]{3,2,1,0:T(8,128)S(1)} %bitcast.3), channel_id=1, source_target_pairs={{0,0},{16,256},{32,32},{48,288},{64,64},{80,320},{96,96},{112,352}... | collective-permute-start | bytes 1572872 | tf_op jit(solution)/shard_map/ppermute | solution.py:232
  62.3 7.9 %collective-permute-start.13 = (f32[8,8,128]{2,1,0:T(8,128)S(1)}, f32[8,8,128]{2,1,0:T(8,128)S(1)}, u32[]{:S(2)}, u32[]{:S(2)}) collective-permute-start(f32[8,8,128]{2,1,0:T(8,128)S(1)} %get-tuple-element.27), channel_id=1, source_target_pairs={{0,32},{16,48},{32,0},{48,16},{64,96},{80,112},{96,64},{112,80},{1... | collective-permute-start | bytes 98312 | tf_op jit(solution)/shard_map/ppermute | solution.py:233
  70.3 1.3 %gradient_keep.1 = f32[8,8,128]{2,1,0:T(8,128)S(1)} custom-call(f32[128,1536]{1,0:T(8,128)S(1)} %get-tuple-element.18.lt0, f32[128,256]{1,0:T(8,128)S(1)} %get-tuple-element.19.lt1, f32[128,256]{1,0:T(8,128)S(1)} %get-tuple-element.20.lt2, bf16[256,1536]{1,0:T(8,128)(2,1)S(1)} %get-tuple-element.21.rt0, bf16[256,256]{1,0:T(8,128)(2,1)S(1)} %get-tuple-element.22.rt1, ...), custom_call_target="tpu_custom_call" | custom-call | flops 1073741824 | bytes 4194304 | tf_op jit(solution)/shard_map/gradient_keep/pallas_call | solution.py:234
  71.6 10.5 %all_to_all.5 = f32[8,8,128]{2,1,0:T(8,128)S(1)} all-to-all(f32[8,8,128]{2,1,0:T(8,128)S(1)} %add.7), channel_id=1, replica_groups={{0,64,128,192,256,320,384,448},{16,80,144,208,272,336,400,464},{32,96,1..., dimensions={0} | all-to-all | bytes 65536 | tf_op jit(solution)/shard_map/all_to_all | solution.py:244
  82.7 0.8 copy.8
  (25 shorter events, 2.4 us)
Async XLA Ops:
  0.6 9.7 %copy-start = (f32[256,2048]{1,0:T(8,128)S(1)}, f32[256,2048]{1,0:T(8,128)}, u32[]{:S(2)}) copy-start(f32[256,2048]{1,0:T(8,128)} %param.4) | copy-start | bytes 6291460
  0.6 14.9 %copy-start.2 = (f32[1,8,128,128]{3,2,1,0:T(8,128)S(1)}, f32[1,8,128,128]{3,2,1,0:T(8,128)}, u32[]{:S(2)}) copy-start(f32[1,8,128,128]{3,2,1,0:T(8,128)} %param.6) | copy-start | bytes 1572868
  0.7 9.9 %collective-permute-start = (s32[1,2]{1,0:T(1,128)}, s32[1,2]{1,0:T(1,128)S(1)}, u32[]{:S(2)}, u32[]{:S(2)}) collective-permute-start(s32[1,2]{1,0:T(1,128)} %param.7), channel_id=1, source_target_pairs={{0,16},{16,0},{32,48},{48,32},{64,80},{80,64},{96,112},{112,96},{1... | collective-permute-start | bytes 32 | tf_op jit(solution)/shard_map/ppermute | solution.py:161
  10.3 36.1 %copy-start.1 = (f32[8,4096]{1,0:T(8,128)S(1)}, f32[8,4096]{1,0:T(8,128)}, u32[]{:S(2)}) copy-start(f32[8,4096]{1,0:T(8,128)} %coef_ref.5) | copy-start | bytes 393220
  11.1 14.6 %collective-permute-start.5 = (f32[128,256]{1,0:T(8,128)S(1)}, f32[128,256]{1,0:T(8,128)S(1)}, u32[]{:S(2)}, u32[]{:S(2)}) collective-permute-start(f32[128,256]{1,0:T(8,128)S(1)} %pick.1.own0), channel_id=1, source_target_pairs={{0,1},{1,0},{2,3},{3,2},{4,5},{5,4},{6,7},{7,6},{8,9},{9,8},{10,11... | collective-permute-start | bytes 393224 | tf_op jit(solution)/shard_map/ppermute | solution.py:175
  13.0 17.1 %collective-permute-start.1 = (f32[128,256]{1,0:T(8,128)S(1)}, f32[128,256]{1,0:T(8,128)S(1)}, u32[]{:S(2)}, u32[]{:S(2)}) collective-permute-start(f32[128,256]{1,0:T(8,128)S(1)} %pick.1.own0), channel_id=1, source_target_pairs={{0,2},{1,3},{2,0},{3,1},{4,6},{5,7},{6,4},{7,5},{8,10},{9,11},{10,... | collective-permute-start | bytes 393224 | tf_op jit(solution)/shard_map/ppermute | solution.py:177
  15.6 33.2 %collective-permute-start.10 = (f32[1,8,128,128]{3,2,1,0:T(8,128)S(1)}, f32[1,8,128,128]{3,2,1,0:T(8,128)S(1)}, u32[]{:S(2)}, u32[]{:S(2)}) collective-permute-start(f32[1,8,128,128]{3,2,1,0:T(8,128)S(1)} %copy-done.2), channel_id=1, source_target_pairs={{0,0},{16,256},{32,32},{48,288},{64,64},{80,320},{96,96},{112,352}... | collective-permute-start | bytes 1572872 | tf_op jit(solution)/shard_map/ppermute | solution.py:162
  23.8 7.5 %collective-permute-start.2 = (f32[128,256]{1,0:T(8,128)S(1)}, f32[128,256]{1,0:T(8,128)S(1)}, u32[]{:S(2)}, u32[]{:S(2)}) collective-permute-start(f32[128,256]{1,0:T(8,128)S(1)} %pick.1.own0), channel_id=1, source_target_pairs={{0,3},{1,2},{2,1},{3,0},{4,7},{5,6},{6,5},{7,4},{8,11},{9,10},{10,... | collective-permute-start | bytes 393224 | tf_op jit(solution)/shard_map/ppermute | solution.py:176
  25.7 15.3 %collective-permute-start.6 = (f32[256,256]{1,0:T(8,128)S(1)}, f32[256,256]{1,0:T(8,128)S(1)}, u32[]{:S(2)}, u32[]{:S(2)}) collective-permute-start(f32[256,256]{1,0:T(8,128)S(1)} %pad_maximum_fusion), channel_id=1, source_target_pairs={{0,12},{1,13},{2,14},{3,15},{4,8},{5,9},{6,10},{7,11},{8,4},{9,5},... | collective-permute-start | bytes 786440 | tf_op jit(solution)/shard_map/ppermute | solution.py:180
  31.3 11.6 %collective-permute-start.3 = (f32[256,256]{1,0:T(8,128)S(1)}, f32[256,256]{1,0:T(8,128)S(1)}, u32[]{:S(2)}, u32[]{:S(2)}) collective-permute-start(f32[256,256]{1,0:T(8,128)S(1)} %constant_dynamic-update-slice_fusion), channel_id=1, source_target_pairs={{0,4},{1,5},{2,6},{3,7},{4,0},{5,1},{6,2},{7,3},{8,12},{9,13},{10,... | collective-permute-start | bytes 786440 | tf_op jit(solution)/shard_map/ppermute | solution.py:182
  34.4 11.2 %collective-permute-start.8 = (f32[256,256]{1,0:T(8,128)S(1)}, f32[256,256]{1,0:T(8,128)S(1)}, u32[]{:S(2)}, u32[]{:S(2)}) collective-permute-start(f32[256,256]{1,0:T(8,128)S(1)} %pad_maximum_fusion), channel_id=1, source_target_pairs={{0,4},{1,5},{2,6},{3,7},{4,0},{5,1},{6,2},{7,3},{8,12},{9,13},{10,... | collective-permute-start | bytes 786440 | tf_op jit(solution)/shard_map/ppermute | solution.py:181
  36.6 9.8 %collective-permute-start.9 = (f32[256,256]{1,0:T(8,128)S(1)}, f32[256,256]{1,0:T(8,128)S(1)}, u32[]{:S(2)}, u32[]{:S(2)}) collective-permute-start(f32[256,256]{1,0:T(8,128)S(1)} %constant_dynamic-update-slice_fusion), channel_id=1, source_target_pairs={{0,12},{1,13},{2,14},{3,15},{4,8},{5,9},{6,10},{7,11},{8,4},{9,5},... | collective-permute-start | bytes 786440 | tf_op jit(solution)/shard_map/ppermute | solution.py:183
  41.0 7.3 %collective-permute-start.7 = (f32[256,256]{1,0:T(8,128)S(1)}, f32[256,256]{1,0:T(8,128)S(1)}, u32[]{:S(2)}, u32[]{:S(2)}) collective-permute-start(f32[256,256]{1,0:T(8,128)S(1)} %collective-permute-done.6.side0), channel_id=1, source_target_pairs={{0,4},{1,5},{2,6},{3,7},{4,0},{5,1},{6,2},{7,3},{8,12},{9,13},{10,... | collective-permute-start | bytes 786440 | tf_op jit(solution)/shard_map/ppermute | solution.py:184
  42.9 8.3 %collective-permute-start.4 = (f32[256,256]{1,0:T(8,128)S(1)}, f32[256,256]{1,0:T(8,128)S(1)}, u32[]{:S(2)}, u32[]{:S(2)}) collective-permute-start(f32[256,256]{1,0:T(8,128)S(1)} %collective-permute-done.3.near1), channel_id=1, source_target_pairs={{0,12},{1,13},{2,14},{3,15},{4,8},{5,9},{6,10},{7,11},{8,4},{9,5},... | collective-permute-start | bytes 786440 | tf_op jit(solution)/shard_map/ppermute | solution.py:185
  51.8 3.8 %collective-permute-start.11 = (f32[8,128,128]{2,1,0:T(8,128)S(1)}, f32[8,128,128]{2,1,0:T(8,128)S(1)}, u32[]{:S(2)}, u32[]{:S(2)}) collective-permute-start(f32[8,128,128]{2,1,0:T(8,128)S(1)} %get-tuple-element.17.u_ref), channel_id=1, source_target_pairs={{0,16},{16,0},{32,48},{48,32},{64,80},{80,64},{96,112},{112,96},{1... | collective-permute-start | bytes 1572872 | tf_op jit(solution)/shard_map/ppermute | solution.py:220
  56.9 25.8 %collective-permute-start.12 = (f32[1,8,128,128]{3,2,1,0:T(8,128)S(1)}, f32[1,8,128,128]{3,2,1,0:T(8,128)S(1)}, u32[]{:S(2)}, u32[]{:S(2)}) collective-permute-start(f32[1,8,128,128]{3,2,1,0:T(8,128)S(1)} %bitcast.3), channel_id=1, source_target_pairs={{0,0},{16,256},{32,32},{48,288},{64,64},{80,320},{96,96},{112,352}... | collective-permute-start | bytes 1572872 | tf_op jit(solution)/shard_map/ppermute | solution.py:232
  62.3 9.3 %collective-permute-start.13 = (f32[8,8,128]{2,1,0:T(8,128)S(1)}, f32[8,8,128]{2,1,0:T(8,128)S(1)}, u32[]{:S(2)}, u32[]{:S(2)}) collective-permute-start(f32[8,8,128]{2,1,0:T(8,128)S(1)} %get-tuple-element.27), channel_id=1, source_target_pairs={{0,32},{16,48},{32,0},{48,16},{64,96},{80,112},{96,64},{112,80},{1... | collective-permute-start | bytes 98312 | tf_op jit(solution)/shard_map/ppermute | solution.py:233

commit v5 on v4

--- a/solution.py
+++ b/solution.py
@@ -135,12 +135,15 @@
             out_ref[xs * 2 + (pair if j == 0 else 1 - pair)] = block[:, j * 128 : (j + 1) * 128]
 
 
-def send_kernel(u_ref, o_ref, lt0, lt1, lt2, rt0, rt1, rt2, out_ref, hh_ref, ll_ref, r_ref):
+def residual_kernel(u_ref, o_ref, r_ref):
+    for a in range(u_ref.shape[0]):
+        r_ref[a] = u_ref[a] + o_ref[a].T
+
+
+def send_kernel(r_ref, lt0, lt1, lt2, rt0, rt1, rt2, out_ref, hh_ref, ll_ref):
     zh = lax.rem(lax.axis_index("mirror") // NC, NZH)
-    for a in range(u_ref.shape[0]):
-        r = u_ref[a] + o_ref[a].T
-        r_ref[a] = r
-        hi, lo = split(2.0 * r)
+    for a in range(r_ref.shape[0]):
+        hi, lo = split(2.0 * r_ref[a])
         rows = pl.ds(a * 128, 128)
         hh_ref[rows, 0:128] = hi
         hh_ref[rows, 128:256] = hi
@@ -220,15 +223,24 @@
     other = lax.ppermute(u, "mirror", mates)
     eight = shape((NY, naux, nb), f32)
     stacked = shape((naux * nb, 2 * nb), bf16)
-    send, hh, ll, res = pl.pallas_call(
+    res = pl.pallas_call(
+        residual_kernel,
+        out_shape=shape((naux, nb, nb), f32),
+        in_specs=[VMEM] * 2,
+        out_specs=VMEM,
+        compiler_params=params(8),
+        cost_estimate=cost(1 << 17, 1),
+        name="residual",
+    )(u, other)
+    send, hh, ll = pl.pallas_call(
         send_kernel,
-        out_shape=(eight, stacked, stacked, shape((naux, nb, nb), f32)),
-        in_specs=[VMEM] * 8,
-        out_specs=[VMEM] * 4,
+        out_shape=(eight, stacked, stacked),
+        in_specs=[VMEM] * 7,
+        out_specs=[VMEM] * 3,
         compiler_params=params(16),
         cost_estimate=cost(2 * unit, 4),
         name="gradient_send",
-    )(u, other, lt0, lt1, lt2, rt0, rt1, rt2)
+    )(res, lt0, lt1, lt2, rt0, rt1, rt2)
     residual = lax.ppermute(res[None], "mirror", swap_pairs())
     moved = lax.ppermute(send, "mirror", [(m, m ^ NC) for m in range(MIRROR)])
     keep = pl.pallas_call(

time: 84 us -> 84.2 us (level)
  transfers between devices with their start and end apart: 14 -> 14, of which waited for: 5 -> 5; matrix products, arithmetic and copies ran while one was open for 2% -> 2% of each run, Pallas kernels for 4% -> 6%
where the time goes in v5:
time: 84.2 us; the launch traced here: 83.7 us
  starting transfers between devices  57.4 us (68%)
  blocking collectives  10.5 us (12%)
  waiting for transfers between devices  6.35 us (8%)
  Pallas kernels  6.23 us (7%)
  local copies, waits for them, and re-layouts  1.64 us (2%)
  between operations  0.92 us (1%)
    all_to_all x1, blocking collectives, per_device(): lax.all_to_all(keep + moved, 'mirror', 0, 0, tiled=True, axis_index_group...  10.5 us
    ppermute x1, starting transfers between devices, per_device(): mate = lax.ppermute(pair_list, 'mirror', mates)  8.92 us
    ppermute x1, starting transfers between devices, per_device(): work = lax.ppermute(targets, 'mirror', swap_pairs())[0]  8.2 us
    ppermute x1, starting transfers between devices, per_device(): moved = lax.ppermute(send, 'mirror', [(m, m ^ NC) for m in range(MIRROR)])  7.93 us
    ppermute x1, starting transfers between devices, per_device(): residual = lax.ppermute(res[None], 'mirror', swap_pairs())  5.39 us
    ppermute x1, starting transfers between devices, per_device(): side0 = lax.ppermute(early, 'blk', x_trade(3))  4.39 us
    ppermute x1, starting transfers between devices, per_device(): side1 = lax.ppermute(late, 'blk', x_trade(3))  4.39 us
    ppermute x1, starting transfers between devices, per_device(): near1 = lax.ppermute(late, 'blk', x_trade(1))  3.12 us
  transfers between devices with their start and end apart: 14, of which 5 were waited for; matrix products, arithmetic and copies ran while one was open for 2% of the time, Pallas kernels for 6%

profile of v5, /device:TPU:1, one launch (start us, length us, event | category | flops | bytes accessed | tf_op | source)
XLA Modules:
  0.0 83.7 jit_solution(2866467855235220930)
XLA Ops:
  0.7 8.9 %collective-permute-start = (s32[1,2]{1,0:T(1,128)}, s32[1,2]{1,0:T(1,128)S(1)}, u32[]{:S(2)}, u32[]{:S(2)}) collective-permute-start(s32[1,2]{1,0:T(1,128)} %param.7), channel_id=1, source_target_pairs={{0,16},{16,0},{32,48},{48,32},{64,80},{80,64},{96,112},{112,96},{1... | collective-permute-start | bytes 32 | tf_op jit(solution)/shard_map/ppermute | solution.py:164
  9.6 0.7 rev.3.mine_ref
  11.1 1.9 %collective-permute-start.5 = (f32[128,256]{1,0:T(8,128)S(1)}, f32[128,256]{1,0:T(8,128)S(1)}, u32[]{:S(2)}, u32[]{:S(2)}) collective-permute-start(f32[128,256]{1,0:T(8,128)S(1)} %pick.1.own0), channel_id=1, source_target_pairs={{0,1},{1,0},{2,3},{3,2},{4,5},{5,4},{6,7},{7,6},{8,9},{9,8},{10,11... | collective-permute-start | bytes 393224 | tf_op jit(solution)/shard_map/ppermute | solution.py:178
  13.0 2.5 %collective-permute-start.1 = (f32[128,256]{1,0:T(8,128)S(1)}, f32[128,256]{1,0:T(8,128)S(1)}, u32[]{:S(2)}, u32[]{:S(2)}) collective-permute-start(f32[128,256]{1,0:T(8,128)S(1)} %pick.1.own0), channel_id=1, source_target_pairs={{0,2},{1,3},{2,0},{3,1},{4,6},{5,7},{6,4},{7,5},{8,10},{9,11},{10,... | collective-permute-start | bytes 393224 | tf_op jit(solution)/shard_map/ppermute | solution.py:180
  15.6 8.2 %collective-permute-start.10 = (f32[1,8,128,128]{3,2,1,0:T(8,128)S(1)}, f32[1,8,128,128]{3,2,1,0:T(8,128)S(1)}, u32[]{:S(2)}, u32[]{:S(2)}) collective-permute-start(f32[1,8,128,128]{3,2,1,0:T(8,128)S(1)} %copy-done.2), channel_id=1, source_target_pairs={{0,0},{16,256},{32,32},{48,288},{64,64},{80,320},{96,96},{112,352}... | collective-permute-start | bytes 1572872 | tf_op jit(solution)/shard_map/ppermute | solution.py:165
  23.8 1.9 %collective-permute-start.2 = (f32[128,256]{1,0:T(8,128)S(1)}, f32[128,256]{1,0:T(8,128)S(1)}, u32[]{:S(2)}, u32[]{:S(2)}) collective-permute-start(f32[128,256]{1,0:T(8,128)S(1)} %pick.1.own0), channel_id=1, source_target_pairs={{0,3},{1,2},{2,1},{3,0},{4,7},{5,6},{6,5},{7,4},{8,11},{9,10},{10,... | collective-permute-start | bytes 393224 | tf_op jit(solution)/shard_map/ppermute | solution.py:179
  25.7 4.4 %collective-permute-start.6 = (f32[256,256]{1,0:T(8,128)S(1)}, f32[256,256]{1,0:T(8,128)S(1)}, u32[]{:S(2)}, u32[]{:S(2)}) collective-permute-start(f32[256,256]{1,0:T(8,128)S(1)} %pad_maximum_fusion), channel_id=1, source_target_pairs={{0,12},{1,13},{2,14},{3,15},{4,8},{5,9},{6,10},{7,11},{8,4},{9,5},... | collective-permute-start | bytes 786440 | tf_op jit(solution)/shard_map/ppermute | solution.py:183
  30.2 1.1 %collective-permute-done.2.own3 = f32[128,256]{1,0:T(8,128)S(1)} collective-permute-done((f32[128,256]{1,0:T(8,128)S(1)}, f32[128,256]{1,0:T(8,128)S(1)}, u32[]{:S(2)}, u32[]{:S(2)}) %collective-permute-start.2) | collective-permute-done | bytes 131104 | tf_op jit(solution)/shard_map/ppermute | solution.py:179
  31.3 3.1 %collective-permute-start.3 = (f32[256,256]{1,0:T(8,128)S(1)}, f32[256,256]{1,0:T(8,128)S(1)}, u32[]{:S(2)}, u32[]{:S(2)}) collective-permute-start(f32[256,256]{1,0:T(8,128)S(1)} %constant_dynamic-update-slice_fusion), channel_id=1, source_target_pairs={{0,4},{1,5},{2,6},{3,7},{4,0},{5,1},{6,2},{7,3},{8,12},{9,13},{10,... | collective-permute-start | bytes 786440 | tf_op jit(solution)/shard_map/ppermute | solution.py:185
  34.4 2.2 %collective-permute-start.8 = (f32[256,256]{1,0:T(8,128)S(1)}, f32[256,256]{1,0:T(8,128)S(1)}, u32[]{:S(2)}, u32[]{:S(2)}) collective-permute-start(f32[256,256]{1,0:T(8,128)S(1)} %pad_maximum_fusion), channel_id=1, source_target_pairs={{0,4},{1,5},{2,6},{3,7},{4,0},{5,1},{6,2},{7,3},{8,12},{9,13},{10,... | collective-permute-start | bytes 786440 | tf_op jit(solution)/shard_map/ppermute | solution.py:184
  36.6 4.4 %collective-permute-start.9 = (f32[256,256]{1,0:T(8,128)S(1)}, f32[256,256]{1,0:T(8,128)S(1)}, u32[]{:S(2)}, u32[]{:S(2)}) collective-permute-start(f32[256,256]{1,0:T(8,128)S(1)} %constant_dynamic-update-slice_fusion), channel_id=1, source_target_pairs={{0,12},{1,13},{2,14},{3,15},{4,8},{5,9},{6,10},{7,11},{8,4},{9,5},... | collective-permute-start | bytes 786440 | tf_op jit(solution)/shard_map/ppermute | solution.py:186
  41.0 1.9 %collective-permute-start.7 = (f32[256,256]{1,0:T(8,128)S(1)}, f32[256,256]{1,0:T(8,128)S(1)}, u32[]{:S(2)}, u32[]{:S(2)}) collective-permute-start(f32[256,256]{1,0:T(8,128)S(1)} %collective-permute-done.6.side0), channel_id=1, source_target_pairs={{0,4},{1,5},{2,6},{3,7},{4,0},{5,1},{6,2},{7,3},{8,12},{9,13},{10,... | collective-permute-start | bytes 786440 | tf_op jit(solution)/shard_map/ppermute | solution.py:187
  42.9 2.7 %collective-permute-start.4 = (f32[256,256]{1,0:T(8,128)S(1)}, f32[256,256]{1,0:T(8,128)S(1)}, u32[]{:S(2)}, u32[]{:S(2)}) collective-permute-start(f32[256,256]{1,0:T(8,128)S(1)} %collective-permute-done.3.near1), channel_id=1, source_target_pairs={{0,12},{1,13},{2,14},{3,15},{4,8},{5,9},{6,10},{7,11},{8,4},{9,5},... | collective-permute-start | bytes 786440 | tf_op jit(solution)/shard_map/ppermute | solution.py:188
  45.7 0.7 collective-permute-done.9.side1
  46.4 1.9 %fit_first.1 = (f32[1024,256]{1,0:T(8,128)S(1)}, f32[128,1536]{1,0:T(8,128)S(1)}, bf16[256,1536]{1,0:T(8,128)(2,1)S(1)}) custom-call(f32[128,256]{1,0:T(8,128)S(1)} %pick.1.own0, f32[128,256]{1,0:T(8,128)S(1)} %collective-permute-done.5.own1, f32[128,256]{1,0:T(8,128)S(1)} %collective-permute-done.1.own2, f32[128,256]{1,0:T(8,128)S(1)} %collective-permute-done.2.own3, ...), custom_call_target="tpu_custom_call" | custom-call | flops 1610612736 | bytes 5242880 | tf_op jit(solution)/shard_map/fit_first/pallas_call | solution.py:192
  48.8 2.5 %collective-permute-done.4.far1 = f32[256,256]{1,0:T(8,128)S(1)} collective-permute-done((f32[256,256]{1,0:T(8,128)S(1)}, f32[256,256]{1,0:T(8,128)S(1)}, u32[]{:S(2)}, u32[]{:S(2)}) %collective-permute-start.4) | collective-permute-done | bytes 262176 | tf_op jit(solution)/shard_map/ppermute | solution.py:188
  51.8 1.9 %collective-permute-start.11 = (f32[8,128,128]{2,1,0:T(8,128)S(1)}, f32[8,128,128]{2,1,0:T(8,128)S(1)}, u32[]{:S(2)}, u32[]{:S(2)}) collective-permute-start(f32[8,128,128]{2,1,0:T(8,128)S(1)} %get-tuple-element.16.u_ref), channel_id=1, source_target_pairs={{0,16},{16,0},{32,48},{48,32},{64,80},{80,64},{96,112},{112,96},{1... | collective-permute-start | bytes 1572872 | tf_op jit(solution)/shard_map/ppermute | solution.py:223
  53.7 1.9 %collective-permute-done.11.o_ref = f32[8,128,128]{2,1,0:T(8,128)S(1)} collective-permute-done((f32[8,128,128]{2,1,0:T(8,128)S(1)}, f32[8,128,128]{2,1,0:T(8,128)S(1)}, u32[]{:S(2)}, u32[]{:S(2)}) %collective-permute-start.11) | collective-permute-done | bytes 524320 | tf_op jit(solution)/shard_map/ppermute | solution.py:223
  55.8 5.4 %collective-permute-start.12 = (f32[1,8,128,128]{3,2,1,0:T(8,128)S(1)}, f32[1,8,128,128]{3,2,1,0:T(8,128)S(1)}, u32[]{:S(2)}, u32[]{:S(2)}) collective-permute-start(f32[1,8,128,128]{3,2,1,0:T(8,128)S(1)} %bitcast.2), channel_id=1, source_target_pairs={{0,0},{16,256},{32,32},{48,288},{64,64},{80,320},{96,96},{112,352}... | collective-permute-start | bytes 1572872 | tf_op jit(solution)/shard_map/ppermute | solution.py:244
  61.2 1.3 %gradient_send.1 = (f32[8,8,128]{2,1,0:T(8,128)S(1)}, bf16[1024,256]{1,0:T(8,128)(2,1)S(1)}, bf16[1024,256]{1,0:T(8,128)(2,1)S(1)}) custom-call(f32[8,128,128]{2,1,0:T(8,128)S(1)} %residual.1.r_ref, f32[128,1536]{1,0:T(8,128)S(1)} %get-tuple-element.17.lt0, f32[128,256]{1,0:T(8,128)S(1)} %get-tuple-element.18.lt1, f32[128,256]{1,0:T(8,128)S(1)} %get-tuple-element.19.lt2, ...), custom_call_target="tpu_custom_call" | custom-call | flops 1073741824 | bytes 4194304 | tf_op jit(solution)/shard_map/gradient_send/pallas_call | solution.py:235
  62.5 7.9 %collective-permute-start.13 = (f32[8,8,128]{2,1,0:T(8,128)S(1)}, f32[8,8,128]{2,1,0:T(8,128)S(1)}, u32[]{:S(2)}, u32[]{:S(2)}) collective-permute-start(f32[8,8,128]{2,1,0:T(8,128)S(1)} %get-tuple-element.25), channel_id=1, source_target_pairs={{0,32},{16,48},{32,0},{48,16},{64,96},{80,112},{96,64},{112,80},{1... | collective-permute-start | bytes 98312 | tf_op jit(solution)/shard_map/ppermute | solution.py:245
  70.4 1.3 %gradient_keep.1 = f32[8,8,128]{2,1,0:T(8,128)S(1)} custom-call(f32[128,1536]{1,0:T(8,128)S(1)} %get-tuple-element.17.lt0, f32[128,256]{1,0:T(8,128)S(1)} %get-tuple-element.18.lt1, f32[128,256]{1,0:T(8,128)S(1)} %get-tuple-element.19.lt2, bf16[256,1536]{1,0:T(8,128)(2,1)S(1)} %get-tuple-element.20.rt0, bf16[256,256]{1,0:T(8,128)(2,1)S(1)} %get-tuple-element.21.rt1, ...), custom_call_target="tpu_custom_call" | custom-call | flops 1073741824 | bytes 4194304 | tf_op jit(solution)/shard_map/gradient_keep/pallas_call | solution.py:246
  71.8 10.5 %all_to_all.5 = f32[8,8,128]{2,1,0:T(8,128)S(1)} all-to-all(f32[8,8,128]{2,1,0:T(8,128)S(1)} %add.7), channel_id=1, replica_groups={{0,64,128,192,256,320,384,448},{16,80,144,208,272,336,400,464},{32,96,1..., dimensions={0} | all-to-all | bytes 65536 | tf_op jit(solution)/shard_map/all_to_all | solution.py:256
  82.9 0.8 copy.8
  (26 shorter events, 2.6 us)
Async XLA Ops:
  0.6 9.7 %copy-start = (f32[256,2048]{1,0:T(8,128)S(1)}, f32[256,2048]{1,0:T(8,128)}, u32[]{:S(2)}) copy-start(f32[256,2048]{1,0:T(8,128)} %param.4) | copy-start | bytes 6291460
  0.6 14.9 %copy-start.2 = (f32[1,8,128,128]{3,2,1,0:T(8,128)S(1)}, f32[1,8,128,128]{3,2,1,0:T(8,128)}, u32[]{:S(2)}) copy-start(f32[1,8,128,128]{3,2,1,0:T(8,128)} %param.6) | copy-start | bytes 1572868
  0.7 9.9 %collective-permute-start = (s32[1,2]{1,0:T(1,128)}, s32[1,2]{1,0:T(1,128)S(1)}, u32[]{:S(2)}, u32[]{:S(2)}) collective-permute-start(s32[1,2]{1,0:T(1,128)} %param.7), channel_id=1, source_target_pairs={{0,16},{16,0},{32,48},{48,32},{64,80},{80,64},{96,112},{112,96},{1... | collective-permute-start | bytes 32 | tf_op jit(solution)/shard_map/ppermute | solution.py:164
  10.3 36.1 %copy-start.1 = (f32[8,4096]{1,0:T(8,128)S(1)}, f32[8,4096]{1,0:T(8,128)}, u32[]{:S(2)}) copy-start(f32[8,4096]{1,0:T(8,128)} %coef_ref.5) | copy-start | bytes 393220
  11.1 14.6 %collective-permute-start.5 = (f32[128,256]{1,0:T(8,128)S(1)}, f32[128,256]{1,0:T(8,128)S(1)}, u32[]{:S(2)}, u32[]{:S(2)}) collective-permute-start(f32[128,256]{1,0:T(8,128)S(1)} %pick.1.own0), channel_id=1, source_target_pairs={{0,1},{1,0},{2,3},{3,2},{4,5},{5,4},{6,7},{7,6},{8,9},{9,8},{10,11... | collective-permute-start | bytes 393224 | tf_op jit(solution)/shard_map/ppermute | solution.py:178
  13.0 17.1 %collective-permute-start.1 = (f32[128,256]{1,0:T(8,128)S(1)}, f32[128,256]{1,0:T(8,128)S(1)}, u32[]{:S(2)}, u32[]{:S(2)}) collective-permute-start(f32[128,256]{1,0:T(8,128)S(1)} %pick.1.own0), channel_id=1, source_target_pairs={{0,2},{1,3},{2,0},{3,1},{4,6},{5,7},{6,4},{7,5},{8,10},{9,11},{10,... | collective-permute-start | bytes 393224 | tf_op jit(solution)/shard_map/ppermute | solution.py:180
  15.6 33.2 %collective-permute-start.10 = (f32[1,8,128,128]{3,2,1,0:T(8,128)S(1)}, f32[1,8,128,128]{3,2,1,0:T(8,128)S(1)}, u32[]{:S(2)}, u32[]{:S(2)}) collective-permute-start(f32[1,8,128,128]{3,2,1,0:T(8,128)S(1)} %copy-done.2), channel_id=1, source_target_pairs={{0,0},{16,256},{32,32},{48,288},{64,64},{80,320},{96,96},{112,352}... | collective-permute-start | bytes 1572872 | tf_op jit(solution)/shard_map/ppermute | solution.py:165
  23.8 7.5 %collective-permute-start.2 = (f32[128,256]{1,0:T(8,128)S(1)}, f32[128,256]{1,0:T(8,128)S(1)}, u32[]{:S(2)}, u32[]{:S(2)}) collective-permute-start(f32[128,256]{1,0:T(8,128)S(1)} %pick.1.own0), channel_id=1, source_target_pairs={{0,3},{1,2},{2,1},{3,0},{4,7},{5,6},{6,5},{7,4},{8,11},{9,10},{10,... | collective-permute-start | bytes 393224 | tf_op jit(solution)/shard_map/ppermute | solution.py:179
  25.7 15.3 %collective-permute-start.6 = (f32[256,256]{1,0:T(8,128)S(1)}, f32[256,256]{1,0:T(8,128)S(1)}, u32[]{:S(2)}, u32[]{:S(2)}) collective-permute-start(f32[256,256]{1,0:T(8,128)S(1)} %pad_maximum_fusion), channel_id=1, source_target_pairs={{0,12},{1,13},{2,14},{3,15},{4,8},{5,9},{6,10},{7,11},{8,4},{9,5},... | collective-permute-start | bytes 786440 | tf_op jit(solution)/shard_map/ppermute | solution.py:183
  31.3 11.6 %collective-permute-start.3 = (f32[256,256]{1,0:T(8,128)S(1)}, f32[256,256]{1,0:T(8,128)S(1)}, u32[]{:S(2)}, u32[]{:S(2)}) collective-permute-start(f32[256,256]{1,0:T(8,128)S(1)} %constant_dynamic-update-slice_fusion), channel_id=1, source_target_pairs={{0,4},{1,5},{2,6},{3,7},{4,0},{5,1},{6,2},{7,3},{8,12},{9,13},{10,... | collective-permute-start | bytes 786440 | tf_op jit(solution)/shard_map/ppermute | solution.py:185
  34.4 11.2 %collective-permute-start.8 = (f32[256,256]{1,0:T(8,128)S(1)}, f32[256,256]{1,0:T(8,128)S(1)}, u32[]{:S(2)}, u32[]{:S(2)}) collective-permute-start(f32[256,256]{1,0:T(8,128)S(1)} %pad_maximum_fusion), channel_id=1, source_target_pairs={{0,4},{1,5},{2,6},{3,7},{4,0},{5,1},{6,2},{7,3},{8,12},{9,13},{10,... | collective-permute-start | bytes 786440 | tf_op jit(solution)/shard_map/ppermute | solution.py:184
  36.6 9.8 %collective-permute-start.9 = (f32[256,256]{1,0:T(8,128)S(1)}, f32[256,256]{1,0:T(8,128)S(1)}, u32[]{:S(2)}, u32[]{:S(2)}) collective-permute-start(f32[256,256]{1,0:T(8,128)S(1)} %constant_dynamic-update-slice_fusion), channel_id=1, source_target_pairs={{0,12},{1,13},{2,14},{3,15},{4,8},{5,9},{6,10},{7,11},{8,4},{9,5},... | collective-permute-start | bytes 786440 | tf_op jit(solution)/shard_map/ppermute | solution.py:186
  41.0 7.3 %collective-permute-start.7 = (f32[256,256]{1,0:T(8,128)S(1)}, f32[256,256]{1,0:T(8,128)S(1)}, u32[]{:S(2)}, u32[]{:S(2)}) collective-permute-start(f32[256,256]{1,0:T(8,128)S(1)} %collective-permute-done.6.side0), channel_id=1, source_target_pairs={{0,4},{1,5},{2,6},{3,7},{4,0},{5,1},{6,2},{7,3},{8,12},{9,13},{10,... | collective-permute-start | bytes 786440 | tf_op jit(solution)/shard_map/ppermute | solution.py:187
  42.9 8.3 %collective-permute-start.4 = (f32[256,256]{1,0:T(8,128)S(1)}, f32[256,256]{1,0:T(8,128)S(1)}, u32[]{:S(2)}, u32[]{:S(2)}) collective-permute-start(f32[256,256]{1,0:T(8,128)S(1)} %collective-permute-done.3.near1), channel_id=1, source_target_pairs={{0,12},{1,13},{2,14},{3,15},{4,8},{5,9},{6,10},{7,11},{8,4},{9,5},... | collective-permute-start | bytes 786440 | tf_op jit(solution)/shard_map/ppermute | solution.py:188
  51.8 3.8 %collective-permute-start.11 = (f32[8,128,128]{2,1,0:T(8,128)S(1)}, f32[8,128,128]{2,1,0:T(8,128)S(1)}, u32[]{:S(2)}, u32[]{:S(2)}) collective-permute-start(f32[8,128,128]{2,1,0:T(8,128)S(1)} %get-tuple-element.16.u_ref), channel_id=1, source_target_pairs={{0,16},{16,0},{32,48},{48,32},{64,80},{80,64},{96,112},{112,96},{1... | collective-permute-start | bytes 1572872 | tf_op jit(solution)/shard_map/ppermute | solution.py:223
  55.8 27.1 %collective-permute-start.12 = (f32[1,8,128,128]{3,2,1,0:T(8,128)S(1)}, f32[1,8,128,128]{3,2,1,0:T(8,128)S(1)}, u32[]{:S(2)}, u32[]{:S(2)}) collective-permute-start(f32[1,8,128,128]{3,2,1,0:T(8,128)S(1)} %bitcast.2), channel_id=1, source_target_pairs={{0,0},{16,256},{32,32},{48,288},{64,64},{80,320},{96,96},{112,352}... | collective-permute-start | bytes 1572872 | tf_op jit(solution)/shard_map/ppermute | solution.py:244
  62.5 9.3 %collective-permute-start.13 = (f32[8,8,128]{2,1,0:T(8,128)S(1)}, f32[8,8,128]{2,1,0:T(8,128)S(1)}, u32[]{:S(2)}, u32[]{:S(2)}) collective-permute-start(f32[8,8,128]{2,1,0:T(8,128)S(1)} %get-tuple-element.25), channel_id=1, source_target_pairs={{0,32},{16,48},{32,0},{48,16},{64,96},{80,112},{96,64},{112,80},{1... | collective-permute-start | bytes 98312 | tf_op jit(solution)/shard_map/ppermute | solution.py:245

commit v6 on v5

--- a/solution.py
+++ b/solution.py
@@ -11,6 +11,7 @@
 HALF = MIRROR // 2
 bf16, f32 = jnp.bfloat16, jnp.float32
 VMEM = pl.BlockSpec(memory_space=pltpu.VMEM)
+ANY = pl.BlockSpec(memory_space=pl.ANY)
 SMEM = pl.BlockSpec(memory_space=pltpu.SMEM)
 
 
@@ -157,6 +158,13 @@
     blocks(zh, (lt0, lt1, lt2), (rt0, rt1, rt2), out_ref, hh_ref, ll_ref)
 
 
+def finish_kernel(s_ref, back_ref, out_ref, residual_ref, sem):
+    copy = pltpu.make_async_copy(back_ref, residual_ref, sem)
+    copy.start()
+    out_ref[...] = jnp.sum(s_ref[...], axis=0)
+    copy.wait()
+
+
 def per_device(colloc, coeffs, targets, pair_list):
     naux, nb = targets.shape[1], targets.shape[2]
     shape = jax.ShapeDtypeStruct
@@ -254,7 +262,17 @@
     )(lt0, lt1, lt2, rt0, rt1, rt2, hh, ll)
     y_groups = [[(y * NZH + h) * NC + c for y in range(NY)] for h in range(NZH) for c in range(NC)]
     spread = lax.all_to_all(keep + moved, "mirror", 0, 0, tiled=True, axis_index_groups=y_groups)
-    return residual, jnp.sum(spread, axis=0)
+    gradient, residual = pl.pallas_call(
+        finish_kernel,
+        out_shape=(shape((naux, nb), f32), shape(residual.shape, f32)),
+        in_specs=[VMEM, ANY],
+        out_specs=[VMEM, ANY],
+        scratch_shapes=[pltpu.SemaphoreType.DMA],
+        compiler_params=params(8),
+        cost_estimate=cost(1 << 17, 1),
+        name="finish",
+    )(spread, residual)
+    return residual, gradient
 
 
 def solution(mesh):

time: 84.2 us -> 84.8 us (level)
  Pallas kernels: 6.23 us -> 7.62 us
    pallas_call x0 -> x1, Pallas kernels: none -> 1.39 us  [per_device(): pl.pallas_call(finish_kernel, out_shape=(shape((naux, nb), f32), shape(re...]
    ppermute x1, starting transfers between devices: 1.92 us -> 3.06 us  [per_device(): far0 = lax.ppermute(side0, 'blk', x_trade(1))]
    ppermute x1, waiting for transfers between devices: 0.01 us -> 0.87 us  [per_device(): near0 = lax.ppermute(early, 'blk', x_trade(1))]
  transfers between devices with their start and end apart: 14 -> 14, of which waited for: 5 -> 6; matrix products, arithmetic and copies ran while one was open for 2% -> 1% of each run, Pallas kernels for 6% -> 6%
where the time goes in v6:
time: 84.8 us; the launch traced here: 84.3 us
  starting transfers between devices  58.1 us (69%)
  blocking collectives  10.5 us (12%)
  Pallas kernels  7.62 us (9%)
  waiting for transfers between devices  6.3 us (7%)
  between operations  0.91 us (1%)
  local copies, waits for them, and re-layouts  0.85 us (1%)
    all_to_all x1, blocking collectives, per_device(): lax.all_to_all(keep + moved, 'mirror', 0, 0, tiled=True, axis_index_group...  10.5 us
    ppermute x1, starting transfers between devices, per_device(): mate = lax.ppermute(pair_list, 'mirror', mates)  8.92 us
    ppermute x1, starting transfers between devices, per_device(): work = lax.ppermute(targets, 'mirror', swap_pairs())[0]  8.2 us
    ppermute x1, starting transfers between devices, per_device(): moved = lax.ppermute(send, 'mirror', [(m, m ^ NC) for m in range(MIRROR)])  7.93 us
    ppermute x1, starting transfers between devices, per_device(): residual = lax.ppermute(res[None], 'mirror', swap_pairs())  5.45 us
    ppermute x1, starting transfers between devices, per_device(): side0 = lax.ppermute(early, 'blk', x_trade(3))  4.39 us
    ppermute x1, starting transfers between devices, per_device(): side1 = lax.ppermute(late, 'blk', x_trade(3))  3.72 us
    ppermute x1, starting transfers between devices, per_device(): near1 = lax.ppermute(late, 'blk', x_trade(1))  3.12 us
  transfers between devices with their start and end apart: 14, of which 6 were waited for; matrix products, arithmetic and copies ran while one was open for 1% of the time, Pallas kernels for 6%

profile of v6, /device:TPU:1, one launch (start us, length us, event | category | flops | bytes accessed | tf_op | source)
XLA Modules:
  0.0 84.3 jit_solution(13444437474780075510)
XLA Ops:
  0.7 8.9 %collective-permute-start = (s32[1,2]{1,0:T(1,128)}, s32[1,2]{1,0:T(1,128)S(1)}, u32[]{:S(2)}, u32[]{:S(2)}) collective-permute-start(s32[1,2]{1,0:T(1,128)} %param.7), channel_id=1, source_target_pairs={{0,16},{16,0},{32,48},{48,32},{64,80},{80,64},{96,112},{112,96},{1... | collective-permute-start | bytes 32 | tf_op jit(solution)/shard_map/ppermute | solution.py:172
  9.6 0.7 rev.3.mine_ref
  11.1 1.9 %collective-permute-start.1 = (f32[128,256]{1,0:T(8,128)S(1)}, f32[128,256]{1,0:T(8,128)S(1)}, u32[]{:S(2)}, u32[]{:S(2)}) collective-permute-start(f32[128,256]{1,0:T(8,128)S(1)} %pick.1.own0), channel_id=1, source_target_pairs={{0,1},{1,0},{2,3},{3,2},{4,5},{5,4},{6,7},{7,6},{8,9},{9,8},{10,11... | collective-permute-start | bytes 393224 | tf_op jit(solution)/shard_map/ppermute | solution.py:186
  13.0 2.5 %collective-permute-start.2 = (f32[128,256]{1,0:T(8,128)S(1)}, f32[128,256]{1,0:T(8,128)S(1)}, u32[]{:S(2)}, u32[]{:S(2)}) collective-permute-start(f32[128,256]{1,0:T(8,128)S(1)} %pick.1.own0), channel_id=1, source_target_pairs={{0,2},{1,3},{2,0},{3,1},{4,6},{5,7},{6,4},{7,5},{8,10},{9,11},{10,... | collective-permute-start | bytes 393224 | tf_op jit(solution)/shard_map/ppermute | solution.py:188
  15.6 8.2 %collective-permute-start.10 = (f32[1,8,128,128]{3,2,1,0:T(8,128)S(1)}, f32[1,8,128,128]{3,2,1,0:T(8,128)S(1)}, u32[]{:S(2)}, u32[]{:S(2)}) collective-permute-start(f32[1,8,128,128]{3,2,1,0:T(8,128)S(1)} %copy-done.2), channel_id=1, source_target_pairs={{0,0},{16,256},{32,32},{48,288},{64,64},{80,320},{96,96},{112,352}... | collective-permute-start | bytes 1572872 | tf_op jit(solution)/shard_map/ppermute | solution.py:173
  23.8 1.9 %collective-permute-start.3 = (f32[128,256]{1,0:T(8,128)S(1)}, f32[128,256]{1,0:T(8,128)S(1)}, u32[]{:S(2)}, u32[]{:S(2)}) collective-permute-start(f32[128,256]{1,0:T(8,128)S(1)} %pick.1.own0), channel_id=1, source_target_pairs={{0,3},{1,2},{2,1},{3,0},{4,7},{5,6},{6,5},{7,4},{8,11},{9,10},{10,... | collective-permute-start | bytes 393224 | tf_op jit(solution)/shard_map/ppermute | solution.py:187
  25.7 4.4 %collective-permute-start.6 = (f32[256,256]{1,0:T(8,128)S(1)}, f32[256,256]{1,0:T(8,128)S(1)}, u32[]{:S(2)}, u32[]{:S(2)}) collective-permute-start(f32[256,256]{1,0:T(8,128)S(1)} %pad_maximum_fusion), channel_id=1, source_target_pairs={{0,12},{1,13},{2,14},{3,15},{4,8},{5,9},{6,10},{7,11},{8,4},{9,5},... | collective-permute-start | bytes 786440 | tf_op jit(solution)/shard_map/ppermute | solution.py:191
  30.2 1.1 %collective-permute-done.3.own3 = f32[128,256]{1,0:T(8,128)S(1)} collective-permute-done((f32[128,256]{1,0:T(8,128)S(1)}, f32[128,256]{1,0:T(8,128)S(1)}, u32[]{:S(2)}, u32[]{:S(2)}) %collective-permute-start.3) | collective-permute-done | bytes 131104 | tf_op jit(solution)/shard_map/ppermute | solution.py:187
  31.3 3.1 %collective-permute-start.5 = (f32[256,256]{1,0:T(8,128)S(1)}, f32[256,256]{1,0:T(8,128)S(1)}, u32[]{:S(2)}, u32[]{:S(2)}) collective-permute-start(f32[256,256]{1,0:T(8,128)S(1)} %constant_dynamic-update-slice_fusion), channel_id=1, source_target_pairs={{0,4},{1,5},{2,6},{3,7},{4,0},{5,1},{6,2},{7,3},{8,12},{9,13},{10,... | collective-permute-start | bytes 786440 | tf_op jit(solution)/shard_map/ppermute | solution.py:193
  34.4 3.7 %collective-permute-start.7 = (f32[256,256]{1,0:T(8,128)S(1)}, f32[256,256]{1,0:T(8,128)S(1)}, u32[]{:S(2)}, u32[]{:S(2)}) collective-permute-start(f32[256,256]{1,0:T(8,128)S(1)} %constant_dynamic-update-slice_fusion), channel_id=1, source_target_pairs={{0,12},{1,13},{2,14},{3,15},{4,8},{5,9},{6,10},{7,11},{8,4},{9,5},... | collective-permute-start | bytes 786440 | tf_op jit(solution)/shard_map/ppermute | solution.py:194
  38.1 2.2 %collective-permute-start.4 = (f32[256,256]{1,0:T(8,128)S(1)}, f32[256,256]{1,0:T(8,128)S(1)}, u32[]{:S(2)}, u32[]{:S(2)}) collective-permute-start(f32[256,256]{1,0:T(8,128)S(1)} %pad_maximum_fusion), channel_id=1, source_target_pairs={{0,4},{1,5},{2,6},{3,7},{4,0},{5,1},{6,2},{7,3},{8,12},{9,13},{10,... | collective-permute-start | bytes 786440 | tf_op jit(solution)/shard_map/ppermute | solution.py:192
  40.4 3.1 %collective-permute-start.8 = (f32[256,256]{1,0:T(8,128)S(1)}, f32[256,256]{1,0:T(8,128)S(1)}, u32[]{:S(2)}, u32[]{:S(2)}) collective-permute-start(f32[256,256]{1,0:T(8,128)S(1)} %collective-permute-done.6.side0), channel_id=1, source_target_pairs={{0,4},{1,5},{2,6},{3,7},{4,0},{5,1},{6,2},{7,3},{8,12},{9,13},{10,... | collective-permute-start | bytes 786440 | tf_op jit(solution)/shard_map/ppermute | solution.py:195
  43.5 2.8 %collective-permute-start.9 = (f32[256,256]{1,0:T(8,128)S(1)}, f32[256,256]{1,0:T(8,128)S(1)}, u32[]{:S(2)}, u32[]{:S(2)}) collective-permute-start(f32[256,256]{1,0:T(8,128)S(1)} %collective-permute-done.5.near1), channel_id=1, source_target_pairs={{0,12},{1,13},{2,14},{3,15},{4,8},{5,9},{6,10},{7,11},{8,4},{9,5},... | collective-permute-start | bytes 786440 | tf_op jit(solution)/shard_map/ppermute | solution.py:196
  46.3 0.9 %collective-permute-done.4.near0 = f32[256,256]{1,0:T(8,128)S(1)} collective-permute-done((f32[256,256]{1,0:T(8,128)S(1)}, f32[256,256]{1,0:T(8,128)S(1)}, u32[]{:S(2)}, u32[]{:S(2)}) %collective-permute-start.4) | collective-permute-done | bytes 262176 | tf_op jit(solution)/shard_map/ppermute | solution.py:192
  47.1 1.9 %fit_first.1 = (f32[1024,256]{1,0:T(8,128)S(1)}, f32[128,1536]{1,0:T(8,128)S(1)}, bf16[256,1536]{1,0:T(8,128)(2,1)S(1)}) custom-call(f32[128,256]{1,0:T(8,128)S(1)} %pick.1.own0, f32[128,256]{1,0:T(8,128)S(1)} %collective-permute-done.1.own1, f32[128,256]{1,0:T(8,128)S(1)} %collective-permute-done.2.own2, f32[128,256]{1,0:T(8,128)S(1)} %collective-permute-done.3.own3, ...), custom_call_target="tpu_custom_call" | custom-call | flops 1610612736 | bytes 5242880 | tf_op jit(solution)/shard_map/fit_first/pallas_call | solution.py:200
  50.1 1.7 %collective-permute-done.9.far1 = f32[256,256]{1,0:T(8,128)S(1)} collective-permute-done((f32[256,256]{1,0:T(8,128)S(1)}, f32[256,256]{1,0:T(8,128)S(1)}, u32[]{:S(2)}, u32[]{:S(2)}) %collective-permute-start.9) | collective-permute-done | bytes 262176 | tf_op jit(solution)/shard_map/ppermute | solution.py:196
  52.3 1.9 %collective-permute-start.11 = (f32[8,128,128]{2,1,0:T(8,128)S(1)}, f32[8,128,128]{2,1,0:T(8,128)S(1)}, u32[]{:S(2)}, u32[]{:S(2)}) collective-permute-start(f32[8,128,128]{2,1,0:T(8,128)S(1)} %get-tuple-element.24.u_ref), channel_id=1, source_target_pairs={{0,16},{16,0},{32,48},{48,32},{64,80},{80,64},{96,112},{112,96},{1... | collective-permute-start | bytes 1572872 | tf_op jit(solution)/shard_map/ppermute | solution.py:231
  54.2 1.9 %collective-permute-done.11.o_ref = f32[8,128,128]{2,1,0:T(8,128)S(1)} collective-permute-done((f32[8,128,128]{2,1,0:T(8,128)S(1)}, f32[8,128,128]{2,1,0:T(8,128)S(1)}, u32[]{:S(2)}, u32[]{:S(2)}) %collective-permute-start.11) | collective-permute-done | bytes 524320 | tf_op jit(solution)/shard_map/ppermute | solution.py:231
  56.3 5.5 %collective-permute-start.13 = (f32[1,8,128,128]{3,2,1,0:T(8,128)S(1)}, f32[1,8,128,128]{3,2,1,0:T(8,128)S(1)}, u32[]{:S(2)}, u32[]{:S(2)}) collective-permute-start(f32[1,8,128,128]{3,2,1,0:T(8,128)S(1)} %bitcast.2), channel_id=1, source_target_pairs={{0,0},{16,256},{32,32},{48,288},{64,64},{80,320},{96,96},{112,352}... | collective-permute-start | bytes 1572872 | tf_op jit(solution)/shard_map/ppermute | solution.py:252
  61.8 1.3 %gradient_send.1 = (f32[8,8,128]{2,1,0:T(8,128)S(1)}, bf16[1024,256]{1,0:T(8,128)(2,1)S(1)}, bf16[1024,256]{1,0:T(8,128)(2,1)S(1)}) custom-call(f32[8,128,128]{2,1,0:T(8,128)S(1)} %residual.1.r_ref, f32[128,1536]{1,0:T(8,128)S(1)} %get-tuple-element.16.lt0, f32[128,256]{1,0:T(8,128)S(1)} %get-tuple-element.18.lt1, f32[128,256]{1,0:T(8,128)S(1)} %get-tuple-element.20.lt2, ...), custom_call_target="tpu_custom_call" | custom-call | flops 1073741824 | bytes 4194304 | tf_op jit(solution)/shard_map/gradient_send/pallas_call | solution.py:243
  63.1 7.9 %collective-permute-start.12 = (f32[8,8,128]{2,1,0:T(8,128)S(1)}, f32[8,8,128]{2,1,0:T(8,128)S(1)}, u32[]{:S(2)}, u32[]{:S(2)}) collective-permute-start(f32[8,8,128]{2,1,0:T(8,128)S(1)} %get-tuple-element.27), channel_id=1, source_target_pairs={{0,32},{16,48},{32,0},{48,16},{64,96},{80,112},{96,64},{112,80},{1... | collective-permute-start | bytes 98312 | tf_op jit(solution)/shard_map/ppermute | solution.py:253
  71.0 1.3 %gradient_keep.1 = f32[8,8,128]{2,1,0:T(8,128)S(1)} custom-call(f32[128,1536]{1,0:T(8,128)S(1)} %get-tuple-element.16.lt0, f32[128,256]{1,0:T(8,128)S(1)} %get-tuple-element.18.lt1, f32[128,256]{1,0:T(8,128)S(1)} %get-tuple-element.20.lt2, bf16[256,1536]{1,0:T(8,128)(2,1)S(1)} %get-tuple-element.21.rt0, bf16[256,256]{1,0:T(8,128)(2,1)S(1)} %get-tuple-element.22.rt1, ...), custom_call_target="tpu_custom_call" | custom-call | flops 1073741824 | bytes 4194304 | tf_op jit(solution)/shard_map/gradient_keep/pallas_call | solution.py:254
  72.4 10.5 %all_to_all.5.s_ref = f32[8,8,128]{2,1,0:T(8,128)S(1)} all-to-all(f32[8,8,128]{2,1,0:T(8,128)S(1)} %add.7), channel_id=1, replica_groups={{0,64,128,192,256,320,384,448},{16,80,144,208,272,336,400,464},{32,96,1..., dimensions={0} | all-to-all | bytes 65536 | tf_op jit(solution)/shard_map/all_to_all | solution.py:264
  82.9 1.4 %finish.1 = (f32[8,128]{1,0:T(8,128)}, f32[1,8,128,128]{3,2,1,0:T(8,128)}) custom-call(f32[8,8,128]{2,1,0:T(8,128)S(1)} %all_to_all.5.s_ref, f32[1,8,128,128]{3,2,1,0:T(8,128)S(1)} %collective-permute-done.13.back_ref), custom_call_target="tpu_custom_call" | custom-call | flops 131072 | bytes 1048576 | tf_op jit(solution)/shard_map/finish/pallas_call | solution.py:265
  (25 shorter events, 2.6 us)
Async XLA Ops:
  0.6 9.7 %copy-start = (f32[256,2048]{1,0:T(8,128)S(1)}, f32[256,2048]{1,0:T(8,128)}, u32[]{:S(2)}) copy-start(f32[256,2048]{1,0:T(8,128)} %param.4) | copy-start | bytes 6291460
  0.6 14.9 %copy-start.2 = (f32[1,8,128,128]{3,2,1,0:T(8,128)S(1)}, f32[1,8,128,128]{3,2,1,0:T(8,128)}, u32[]{:S(2)}) copy-start(f32[1,8,128,128]{3,2,1,0:T(8,128)} %param.6) | copy-start | bytes 1572868
  0.7 9.9 %collective-permute-start = (s32[1,2]{1,0:T(1,128)}, s32[1,2]{1,0:T(1,128)S(1)}, u32[]{:S(2)}, u32[]{:S(2)}) collective-permute-start(s32[1,2]{1,0:T(1,128)} %param.7), channel_id=1, source_target_pairs={{0,16},{16,0},{32,48},{48,32},{64,80},{80,64},{96,112},{112,96},{1... | collective-permute-start | bytes 32 | tf_op jit(solution)/shard_map/ppermute | solution.py:172
  10.3 36.8 %copy-start.1 = (f32[8,4096]{1,0:T(8,128)S(1)}, f32[8,4096]{1,0:T(8,128)}, u32[]{:S(2)}) copy-start(f32[8,4096]{1,0:T(8,128)} %coef_ref.5) | copy-start | bytes 393220
  11.1 14.6 %collective-permute-start.1 = (f32[128,256]{1,0:T(8,128)S(1)}, f32[128,256]{1,0:T(8,128)S(1)}, u32[]{:S(2)}, u32[]{:S(2)}) collective-permute-start(f32[128,256]{1,0:T(8,128)S(1)} %pick.1.own0), channel_id=1, source_target_pairs={{0,1},{1,0},{2,3},{3,2},{4,5},{5,4},{6,7},{7,6},{8,9},{9,8},{10,11... | collective-permute-start | bytes 393224 | tf_op jit(solution)/shard_map/ppermute | solution.py:186
  13.0 17.1 %collective-permute-start.2 = (f32[128,256]{1,0:T(8,128)S(1)}, f32[128,256]{1,0:T(8,128)S(1)}, u32[]{:S(2)}, u32[]{:S(2)}) collective-permute-start(f32[128,256]{1,0:T(8,128)S(1)} %pick.1.own0), channel_id=1, source_target_pairs={{0,2},{1,3},{2,0},{3,1},{4,6},{5,7},{6,4},{7,5},{8,10},{9,11},{10,... | collective-permute-start | bytes 393224 | tf_op jit(solution)/shard_map/ppermute | solution.py:188
  15.6 34.6 %collective-permute-start.10 = (f32[1,8,128,128]{3,2,1,0:T(8,128)S(1)}, f32[1,8,128,128]{3,2,1,0:T(8,128)S(1)}, u32[]{:S(2)}, u32[]{:S(2)}) collective-permute-start(f32[1,8,128,128]{3,2,1,0:T(8,128)S(1)} %copy-done.2), channel_id=1, source_target_pairs={{0,0},{16,256},{32,32},{48,288},{64,64},{80,320},{96,96},{112,352}... | collective-permute-start | bytes 1572872 | tf_op jit(solution)/shard_map/ppermute | solution.py:173
  23.8 7.5 %collective-permute-start.3 = (f32[128,256]{1,0:T(8,128)S(1)}, f32[128,256]{1,0:T(8,128)S(1)}, u32[]{:S(2)}, u32[]{:S(2)}) collective-permute-start(f32[128,256]{1,0:T(8,128)S(1)} %pick.1.own0), channel_id=1, source_target_pairs={{0,3},{1,2},{2,1},{3,0},{4,7},{5,6},{6,5},{7,4},{8,11},{9,10},{10,... | collective-permute-start | bytes 393224 | tf_op jit(solution)/shard_map/ppermute | solution.py:187
  25.7 14.6 %collective-permute-start.6 = (f32[256,256]{1,0:T(8,128)S(1)}, f32[256,256]{1,0:T(8,128)S(1)}, u32[]{:S(2)}, u32[]{:S(2)}) collective-permute-start(f32[256,256]{1,0:T(8,128)S(1)} %pad_maximum_fusion), channel_id=1, source_target_pairs={{0,12},{1,13},{2,14},{3,15},{4,8},{5,9},{6,10},{7,11},{8,4},{9,5},... | collective-permute-start | bytes 786440 | tf_op jit(solution)/shard_map/ppermute | solution.py:191
  31.3 12.2 %collective-permute-start.5 = (f32[256,256]{1,0:T(8,128)S(1)}, f32[256,256]{1,0:T(8,128)S(1)}, u32[]{:S(2)}, u32[]{:S(2)}) collective-permute-start(f32[256,256]{1,0:T(8,128)S(1)} %constant_dynamic-update-slice_fusion), channel_id=1, source_target_pairs={{0,4},{1,5},{2,6},{3,7},{4,0},{5,1},{6,2},{7,3},{8,12},{9,13},{10,... | collective-permute-start | bytes 786440 | tf_op jit(solution)/shard_map/ppermute | solution.py:193
  34.4 11.8 %collective-permute-start.7 = (f32[256,256]{1,0:T(8,128)S(1)}, f32[256,256]{1,0:T(8,128)S(1)}, u32[]{:S(2)}, u32[]{:S(2)}) collective-permute-start(f32[256,256]{1,0:T(8,128)S(1)} %constant_dynamic-update-slice_fusion), channel_id=1, source_target_pairs={{0,12},{1,13},{2,14},{3,15},{4,8},{5,9},{6,10},{7,11},{8,4},{9,5},... | collective-permute-start | bytes 786440 | tf_op jit(solution)/shard_map/ppermute | solution.py:194
  38.1 9.0 %collective-permute-start.4 = (f32[256,256]{1,0:T(8,128)S(1)}, f32[256,256]{1,0:T(8,128)S(1)}, u32[]{:S(2)}, u32[]{:S(2)}) collective-permute-start(f32[256,256]{1,0:T(8,128)S(1)} %pad_maximum_fusion), channel_id=1, source_target_pairs={{0,4},{1,5},{2,6},{3,7},{4,0},{5,1},{6,2},{7,3},{8,12},{9,13},{10,... | collective-permute-start | bytes 786440 | tf_op jit(solution)/shard_map/ppermute | solution.py:192
  40.4 9.3 %collective-permute-start.8 = (f32[256,256]{1,0:T(8,128)S(1)}, f32[256,256]{1,0:T(8,128)S(1)}, u32[]{:S(2)}, u32[]{:S(2)}) collective-permute-start(f32[256,256]{1,0:T(8,128)S(1)} %collective-permute-done.6.side0), channel_id=1, source_target_pairs={{0,4},{1,5},{2,6},{3,7},{4,0},{5,1},{6,2},{7,3},{8,12},{9,13},{10,... | collective-permute-start | bytes 786440 | tf_op jit(solution)/shard_map/ppermute | solution.py:195
  43.5 8.3 %collective-permute-start.9 = (f32[256,256]{1,0:T(8,128)S(1)}, f32[256,256]{1,0:T(8,128)S(1)}, u32[]{:S(2)}, u32[]{:S(2)}) collective-permute-start(f32[256,256]{1,0:T(8,128)S(1)} %collective-permute-done.5.near1), channel_id=1, source_target_pairs={{0,12},{1,13},{2,14},{3,15},{4,8},{5,9},{6,10},{7,11},{8,4},{9,5},... | collective-permute-start | bytes 786440 | tf_op jit(solution)/shard_map/ppermute | solution.py:196
  52.3 3.8 %collective-permute-start.11 = (f32[8,128,128]{2,1,0:T(8,128)S(1)}, f32[8,128,128]{2,1,0:T(8,128)S(1)}, u32[]{:S(2)}, u32[]{:S(2)}) collective-permute-start(f32[8,128,128]{2,1,0:T(8,128)S(1)} %get-tuple-element.24.u_ref), channel_id=1, source_target_pairs={{0,16},{16,0},{32,48},{48,32},{64,80},{80,64},{96,112},{112,96},{1... | collective-permute-start | bytes 1572872 | tf_op jit(solution)/shard_map/ppermute | solution.py:231
  56.3 26.6 %collective-permute-start.13 = (f32[1,8,128,128]{3,2,1,0:T(8,128)S(1)}, f32[1,8,128,128]{3,2,1,0:T(8,128)S(1)}, u32[]{:S(2)}, u32[]{:S(2)}) collective-permute-start(f32[1,8,128,128]{3,2,1,0:T(8,128)S(1)} %bitcast.2), channel_id=1, source_target_pairs={{0,0},{16,256},{32,32},{48,288},{64,64},{80,320},{96,96},{112,352}... | collective-permute-start | bytes 1572872 | tf_op jit(solution)/shard_map/ppermute | solution.py:252
  63.1 9.3 %collective-permute-start.12 = (f32[8,8,128]{2,1,0:T(8,128)S(1)}, f32[8,8,128]{2,1,0:T(8,128)S(1)}, u32[]{:S(2)}, u32[]{:S(2)}) collective-permute-start(f32[8,8,128]{2,1,0:T(8,128)S(1)} %get-tuple-element.27), channel_id=1, source_target_pairs={{0,32},{16,48},{32,0},{48,16},{64,96},{80,112},{96,64},{112,80},{1... | collective-permute-start | bytes 98312 | tf_op jit(solution)/shard_map/ppermute | solution.py:253
